TPU v7x, 256 devices: a whole 4x4x8 slice. The times are simulated.
256 devices in a mesh: dp: 16 (over z, core), camp: 16 (over x, y).
Axes of the slice: x: 4, y: 4, z: 8, core: 2. Of those that a mesh axis runs over, the one named last changes fastest.
Arguments:
- row_factors: bfloat16 [131072, 32], P('dp'), may hold values from -120 to 120
- col_factors: bfloat16 [1048576, 32], P('camp'), may hold values from -1 to 1
- prices: float32 [1048576], P('camp'), may hold values from 0.05 to 1
- spend_target: float32 [1048576], P('camp'), may hold values from 0.01 to 0.3
- step_sizes: float32 [3], replicated, may hold values from 1 to 4
- eligible: int32 [1024, 32], P('dp'), may hold values from 0 to 8191, as said below
- counts: int32 [1024], P('dp'), may hold values from 16 to 32
Outputs:
- new_prices: float32 [1048576], P('camp')
- row_norms: float32 [131072], P('dp')
Inputs may be any that keep to these rules, and one draw needn't show every extreme that they name: `eligible`: each row block's slots are grouped by owning camp shard (column block // 512), each shard's slots contiguous, the shards in cyclic order; the first group belongs to the row block's leading shard and holds exactly 8 slots, every later group at most 2, and some later group exactly 2; the column blocks of a row block are distinct. Within each aligned run of 64 row blocks one camp shard leads exactly 8 row blocks and no shard leads more.
All inputs are finite; a program needn't handle non-finite values.
Results may differ from a plain program's by a relative error of at most 0.0006.
Values sent between devices are 32-bit elements; how exact they have to be, the bound alone decides.
A program may use at most 64 MiB of HBM per device.

v0:
```python
import jax
import jax.numpy as jnp
from jax import lax
from jax.sharding import PartitionSpec as P

SHARD_MOST = 8
PASSES = 3


SMOOTHING_TEMP = 0.3


def masked_sum(logit_values, live_mask, top_value):
    return jnp.sum(
        jnp.where(live_mask, jnp.exp(logit_values - top_value[:, None, :, None]), 0.0), axis=(1, 3)
    )


def row_normalizer(every_logit, mask_all, leading_logits, mask_lead, lead_rows):
    top_all = jnp.maximum(jnp.max(jnp.where(mask_all, every_logit, -jnp.inf), axis=(1, 3)), 0.0)
    top_lead = jnp.maximum(
        jnp.max(jnp.where(mask_lead, leading_logits, -jnp.inf), axis=(1, 3)), 0.0
    )
    local_top = top_all.at[lead_rows].max(top_lead)
    top_value = lax.pmax(local_top, "camp")
    local_sum = masked_sum(every_logit, mask_all, top_value)
    local_sum = local_sum.at[lead_rows].add(
        masked_sum(leading_logits, mask_lead, top_value[lead_rows])
    )
    sum_value = lax.psum(local_sum, "camp")
    return top_value + jnp.log(sum_value + jnp.exp(-top_value))


def slot_tiles(slot_ids, slot_counts, first_slot, width, keep, col_blocks, own_shard):
    slot_count = slot_ids.shape[1]
    picked = first_slot[:, None] + jnp.arange(width, dtype=jnp.int32)[None, :]
    inside = picked < slot_count
    picked = jnp.minimum(picked, slot_count - 1)
    chosen = jnp.take_along_axis(slot_ids, picked, axis=1)
    valid = (
        inside
        & (chosen // col_blocks == own_shard)
        & (picked < slot_counts[:, None])
        & keep[:, None]
    )
    local_block = jnp.clip(chosen - own_shard * col_blocks, 0, col_blocks - 1)
    return (local_block, valid)


def local(row_factors, col_factors, prices, spend_target, step_sizes, eligible, counts):
    row_blocks = eligible.shape[0]
    slot_count = eligible.shape[1]
    block_rows = row_factors.shape[0] // row_blocks
    factor_rank = row_factors.shape[1]
    col_blocks = col_factors.shape[0] // block_rows
    camp_count = lax.axis_size("camp")
    other_most = (slot_count - SHARD_MOST + camp_count - 2) // (camp_count - 1)
    lead_most = max(max(1, row_blocks // 8), (row_blocks + camp_count - 1) // camp_count)
    own_shard = lax.axis_index("camp")
    owned = eligible // col_blocks == own_shard
    position = lax.broadcasted_iota(jnp.int32, eligible.shape, 1)
    earlier = jnp.min(jnp.where(owned, position, slot_count), axis=1)
    is_led = eligible[:, 0] // col_blocks == own_shard
    row_order = jnp.arange(row_blocks, dtype=jnp.int32)
    lead_rows = jnp.argsort(jnp.where(is_led, row_order, row_order + row_blocks))[:lead_most]
    lead_keep = is_led[lead_rows]
    every_block, valid_all = slot_tiles(
        eligible, counts, earlier, other_most, jnp.logical_not(is_led), col_blocks, own_shard
    )
    leading_block, valid_lead = slot_tiles(
        eligible[lead_rows],
        counts[lead_rows],
        earlier[lead_rows],
        SHARD_MOST,
        lead_keep,
        col_blocks,
        own_shard,
    )
    col_tiles = col_factors.reshape(col_blocks, block_rows, factor_rank)
    row_tiles = row_factors.reshape(row_blocks, block_rows, factor_rank)
    every_score = jnp.einsum(
        "brk,bmck->bmrc", row_tiles, col_tiles[every_block], preferred_element_type=jnp.float32
    )
    leading_scores = jnp.einsum(
        "brk,bmck->bmrc",
        row_tiles[lead_rows],
        col_tiles[leading_block],
        preferred_element_type=jnp.float32,
    )
    block_index = jnp.arange(col_blocks, dtype=jnp.int32)[None, :]
    selector_all = (
        (every_block.reshape(-1)[:, None] == block_index) & valid_all.reshape(-1)[:, None]
    ).astype(jnp.float32)
    selector_lead = (
        (leading_block.reshape(-1)[:, None] == block_index) & valid_lead.reshape(-1)[:, None]
    ).astype(jnp.float32)
    mask_all = valid_all[:, :, None, None]
    mask_lead = valid_lead[:, :, None, None]
    price = prices
    log_norm = None
    for pass_index in range(PASSES):
        price_block_list = price.reshape(col_blocks, block_rows)
        every_logit = (every_score - price_block_list[every_block][:, :, None, :]) / SMOOTHING_TEMP
        leading_logits = (
            leading_scores - price_block_list[leading_block][:, :, None, :]
        ) / SMOOTHING_TEMP
        log_norm = row_normalizer(every_logit, mask_all, leading_logits, mask_lead, lead_rows)
        assign_all = jnp.where(mask_all, jnp.exp(every_logit - log_norm[:, None, :, None]), 0.0)
        assign_lead = jnp.where(
            mask_lead, jnp.exp(leading_logits - log_norm[lead_rows][:, None, :, None]), 0.0
        )
        part_all = jnp.sum(assign_all, axis=2).reshape(-1, block_rows)
        part_lead = jnp.sum(assign_lead, axis=2).reshape(-1, block_rows)
        local_cols = (
            jnp.dot(
                selector_all.T,
                part_all,
                precision=lax.Precision.HIGHEST,
                preferred_element_type=jnp.float32,
            )
            + jnp.dot(
                selector_lead.T,
                part_lead,
                precision=lax.Precision.HIGHEST,
                preferred_element_type=jnp.float32,
            )
        ).reshape(-1)
        colsum = lax.psum(local_cols, "dp")
        price = jnp.maximum(price + step_sizes[pass_index] * (colsum - spend_target), 0.0)
    return (price, log_norm.reshape(-1))


def solution(mesh):
    placed = (P("dp", None), P("camp", None), P("camp"), P("camp"), P(), P("dp", None), P("dp"))
    return jax.shard_map(
        local, mesh=mesh, in_specs=placed, out_specs=(P("camp"), P("dp")), check_vma=False
    )
```

profile of v0, /device:TPU:1, one launch (start us, length us, event | category | flops | bytes accessed | tf_op | source)
XLA Modules:
  0.0 891.7 jit_solution(16439560172082127311)
XLA Ops:
  7.2 0.8 select_reduce_fusion.18
  8.0 1.2 not_bitcast_fusion
  9.2 0.7 add_select_fusion.3
  10.2 1.3 gather_fusion.19
  11.6 0.8 reshape.786
  12.5 2.0 sort.17
  15.9 0.7 gather_fusion.20
  18.5 4.8 copy_bitcast_fusion
  23.3 2.8 gather_fusion.6
  26.2 3.0 gather_fusion
  29.2 1.2 gather_fusion.5
  31.8 0.9 fusion.47
  32.7 6.2 select_reduce_fusion.8
  39.0 3.4 select_reduce_fusion.17
  43.1 61.2 %pmax.21 = f32[64,128]{1,0:T(8,128)S(1)} all-reduce(f32[64,128]{1,0:T(8,128)S(1)} %scatter_custom_fusion), channel_id=1, replica_groups=mesh['dp'=16,'camp'=16] {'camp'}, use_global_device_ids=true, to_apply=%region_5.6 | all-reduce | flops 8192 | bytes 65536 | tf_op jit(solution)/shard_map/pmax | solution.py:25
  104.9 5.6 select_reduce_fusion.5
  110.6 1.5 select_reduce_fusion.14
  112.1 0.7 scatter_fusion
  112.8 55.9 %psum.42 = f32[64,128]{1,0:T(8,128)S(1)} all-reduce(f32[64,128]{1,0:T(8,128)S(1)} %scatter_fusion), channel_id=1, replica_groups=mesh['dp'=16,'camp'=16] {'camp'}, use_global_device_ids=true, to_apply=%region_9.10 | all-reduce | flops 8192 | bytes 65536 | tf_op jit(solution)/shard_map/psum | solution.py:30
  168.7 7.1 select_reduce_fusion.4
  178.1 4.1 select_reduce_fusion.13
  182.8 1.2 fusion.2
  184.6 133.6 %all-reduce.4.cloned.1.call-done = f32[65536]{0:T(1024)} async-done(((f32[65536]{0:T(1024)}), f32[65536]{0:T(1024)}) %all-reduce.4.cloned.1.call-update) | async-done | bytes 262160 | tf_op jit(solution)/shard_map/psum | solution.py:128
  318.2 1.7 fusion.22
  321.1 2.9 select_reduce_fusion.16
  324.1 5.3 select_reduce_fusion.7
  329.4 0.9 scatter_custom_fusion.2
  330.3 60.1 %pmax.22 = f32[64,128]{1,0:T(8,128)S(1)} all-reduce(f32[64,128]{1,0:T(8,128)S(1)} %scatter_custom_fusion.2), channel_id=1, replica_groups=mesh['dp'=16,'camp'=16] {'camp'}, use_global_device_ids=true, to_apply=%region_16.17 | all-reduce | flops 8192 | bytes 65536 | tf_op jit(solution)/shard_map/pmax | solution.py:25
  390.9 5.6 select_reduce_fusion.3
  396.6 1.5 select_reduce_fusion.12
  398.8 55.8 %psum.44 = f32[64,128]{1,0:T(8,128)S(1)} all-reduce(f32[64,128]{1,0:T(8,128)S(1)} %scatter_fusion.1), channel_id=1, replica_groups=mesh['dp'=16,'camp'=16] {'camp'}, use_global_device_ids=true, to_apply=%region_20.21 | all-reduce | flops 8192 | bytes 65536 | tf_op jit(solution)/shard_map/psum | solution.py:30
  454.7 7.1 select_reduce_fusion.2
  462.4 4.1 select_reduce_fusion.11
  467.0 1.2 fusion.1
  468.3 132.0 %all-reduce.6.cloned.1.call-done = f32[65536]{0:T(1024)} async-done(((f32[65536]{0:T(1024)}), f32[65536]{0:T(1024)}) %all-reduce.6.cloned.1.call-update) | async-done | bytes 262160 | tf_op jit(solution)/shard_map/psum | solution.py:128
  600.3 2.3 add_maximum_fusion.1
  603.8 2.9 select_reduce_fusion.15
  606.7 5.3 select_reduce_fusion.6
  612.1 0.7 scatter_custom_fusion.4
  612.8 60.1 %pmax.23 = f32[64,128]{1,0:T(8,128)S(1)} all-reduce(f32[64,128]{1,0:T(8,128)S(1)} %scatter_custom_fusion.4), channel_id=1, replica_groups=mesh['dp'=16,'camp'=16] {'camp'}, use_global_device_ids=true, to_apply=%region_27.28 | all-reduce | flops 8192 | bytes 65536 | tf_op jit(solution)/shard_map/pmax | solution.py:25
  673.4 5.6 select_reduce_fusion.1
  679.0 1.5 select_reduce_fusion.10
  681.3 56.0 %psum.46 = f32[64,128]{1,0:T(8,128)S(1)} all-reduce(f32[64,128]{1,0:T(8,128)S(1)} %scatter_fusion.2), channel_id=1, replica_groups=mesh['dp'=16,'camp'=16] {'camp'}, use_global_device_ids=true, to_apply=%region_31.32 | all-reduce | flops 8192 | bytes 65536 | tf_op jit(solution)/shard_map/psum | solution.py:30
  737.3 7.1 select_reduce_fusion
  745.0 4.1 select_reduce_fusion.9
  749.6 1.2 fusion
  750.8 132.1 %all-reduce.8.cloned.1.call-done = f32[65536]{0:T(1024)} async-done(((f32[65536]{0:T(1024)}), f32[65536]{0:T(1024)}) %all-reduce.8.cloned.1.call-update) | async-done | bytes 262160 | tf_op jit(solution)/shard_map/psum | solution.py:128
  882.9 2.3 add_maximum_fusion
  (105 shorter events, 16.9 us)
Async XLA Ops:
  7.2 3.0 copy-start
  7.2 311.0 %all-reduce.4.cloned.1.call-start = ((), (), s32[]{:S(2)}) async-start(), calls=%async_computation | async-start | bytes 524288 | tf_op jit(solution)/shard_map/psum | solution.py:128
  11.5 5.7 copy-start.5
  26.1 4.2 copy-start.1
  26.2 4.8 copy-start.7
  32.7 6.2 copy-start.12
  104.9 5.7 copy-start.2
  168.7 8.4 copy-start.11
  175.9 8.1 copy-start.10
  175.9 142.3 %copy-start.6 = (f32[65536]{0:T(1024)S(1)}, f32[65536]{0:T(1024)}, u32[]{:S(2)}) copy-start(f32[65536]{0:T(1024)} %param.10) | copy-start | bytes 786436
  183.9 416.4 %all-reduce.6.cloned.1.call-start = ((), (), s32[]{:S(2)}) async-start(), calls=%async_computation.1 | async-start | bytes 524288 | tf_op jit(solution)/shard_map/psum | solution.py:128
  390.9 5.7 copy-start.3
  461.8 138.5 %copy-start.8 = (f32[65536]{0:T(1024)S(1)}, f32[65536]{0:T(1024)}, u32[]{:S(2)}) copy-start(f32[65536]{0:T(1024)} %all-reduce.4.cloned.1.call-done) | copy-start | bytes 786436
  468.2 414.6 %all-reduce.8.cloned.1.call-start = ((), (), s32[]{:S(2)}) async-start(), calls=%async_computation.2 | async-start | bytes 524288 | tf_op jit(solution)/shard_map/psum | solution.py:128
  673.4 5.6 copy-start.4
  737.3 7.1 copy-start.9
Sparse Core Ops, SparseCore 0:
  184.1 134.0 all-reduce.3
  468.3 131.9 all-reduce.5
  750.9 131.9 all-reduce.7
where the time goes:
time: 893 us; the launch traced here: 892 us
  waiting for transfers between devices  398 us (45%)
  blocking collectives  349 us (39%)
  other arithmetic  88.5 us (10%)
  local copies, waits for them, and re-layouts  27.4 us (3%)
  matrix products  14.5 us (2%)
  between operations  14.3 us (2%)
    psum x3, waiting for transfers between devices, local(): colsum = lax.psum(local_cols, 'dp')  398 us
    pmax x3, blocking collectives, row_normalizer(): top_value = lax.pmax(local_top, 'camp')  181 us
    psum x3, blocking collectives, row_normalizer(): sum_value = lax.psum(local_sum, 'camp')  168 us
    reduce_sum x6, other arithmetic, masked_sum(): jnp.sum(jnp.where(live_mask, jnp.exp(logit_values - top_value[:, None, :,...  21.5 us
    reduce_sum x3, other arithmetic, local(): part_all = jnp.sum(assign_all, axis=2).reshape(-1, block_rows)  21.4 us
  transfers between devices with their start and end apart: 3, of which 3 were waited for; matrix products, arithmetic and copies ran while one was open for 0% of the time, Pallas kernels for 0%

commit v1 on v0

v1 whole, which is shorter than its diff:
```python
import functools
import math

import jax
import jax.numpy as jnp
from jax import lax
from jax.experimental import pallas as pl
from jax.experimental.pallas import tpu as pltpu
from jax.sharding import PartitionSpec as P

MESH = pl.DeviceIdType.MESH
F32 = jnp.float32
BF16 = jnp.bfloat16
BLOCK = 128
RANK = 32
PASSES = 3
LEADS = 8
LEAD_SLOTS = 8
SCALE = math.log2(math.e) / 0.3
LN2 = math.log(2.0)
DEAD = 1e30
GROUP = 4


def pieces(x):
    hi = x.astype(BF16)
    rest = x - hi.astype(F32)
    mid = rest.astype(BF16)
    low = (rest - mid.astype(F32)).astype(BF16)
    return hi, mid, low


def mm(a, b):
    return lax.dot_general(a, b, (((1,), (0,)), ((), ())), preferred_element_type=F32)


def mm_nt(a, b):
    return lax.dot_general(a, b, (((1,), (1,)), ((), ())), preferred_element_type=F32)


def exact_pick(select, x):
    hi, mid, low = pieces(x)
    out = mm(select, jnp.concatenate([hi, mid, low], axis=1))
    return out[:, :BLOCK] + out[:, BLOCK : 2 * BLOCK] + out[:, 2 * BLOCK :]


def slot_index(elig, cnt, own, col_blocks):
    slots, rows = elig.shape
    pos = lax.broadcasted_iota(jnp.int32, elig.shape, 0)
    owned = lax.div(elig, col_blocks) == own
    led = owned[0:1, :]
    first = jnp.min(jnp.where(owned, pos, slots), axis=0, keepdims=True)
    blocks, valids = [], []
    for k in range(2):
        picked = first + k
        chosen = jnp.sum(jnp.where(pos == picked, elig, 0), axis=0, keepdims=True)
        ok = (
            (picked < slots)
            & (lax.div(chosen, col_blocks) == own)
            & (picked < cnt)
            & jnp.logical_not(led)
        )
        blocks.append(jnp.where(ok, chosen - own * col_blocks, 0))
        valids.append(ok.astype(jnp.int32))
    led_f = jnp.broadcast_to(led.astype(F32), (8, rows))
    before = (
        lax.broadcasted_iota(jnp.int32, (rows, rows), 0)
        < lax.broadcasted_iota(jnp.int32, (rows, rows), 1)
    ).astype(F32)
    rank = mm(led_f.astype(BF16), before.astype(BF16))[0:1, :]
    lane = lax.broadcasted_iota(jnp.int32, (LEADS * LEAD_SLOTS, rows), 0)
    hot = jnp.where((rank == lax.rem(lane, LEADS).astype(F32)) & led, 1.0, 0.0)
    row_id = lax.broadcasted_iota(jnp.int32, (8, rows), 1).astype(F32)
    high = lax.div(elig, 128)
    picked = mm_nt(
        jnp.concatenate(
            [
                high.astype(F32),
                (elig - high * 128).astype(F32),
                jnp.broadcast_to(cnt, (8, rows)).astype(F32),
                jnp.ones((8, rows), F32),
                row_id,
            ],
            axis=0,
        ).astype(BF16),
        hot.astype(BF16),
    )
    wide = LEADS * LEAD_SLOTS
    every = picked[0:slots] * 128.0 + picked[slots : 2 * slots]
    slot_of = lax.div(lax.broadcasted_iota(jnp.int32, (slots, wide), 1), LEADS)
    chosen = jnp.sum(
        jnp.where(lax.broadcasted_iota(jnp.int32, (slots, wide), 0) == slot_of, every, 0.0),
        axis=0,
        keepdims=True,
    ).astype(jnp.int32)
    lead_cnt = picked[2 * slots : 2 * slots + 1]
    exists = picked[2 * slots + 8 : 2 * slots + 9] > 0.5
    lead_row = picked[2 * slots + 16 : 2 * slots + 17].astype(jnp.int32)
    ok = exists & (slot_of[0:1].astype(F32) < lead_cnt)
    blocks.append(jnp.where(ok, chosen - own * col_blocks, 0))
    valids.append(ok.astype(jnp.int32))
    blocks.append(jnp.zeros_like(lead_row))
    valids.append(jnp.zeros_like(lead_row))
    place = jnp.where(exists, lead_row, -1)
    return (
        jnp.concatenate(blocks, axis=1),
        jnp.concatenate(valids, axis=1),
        jnp.concatenate([lead_row, place, lead_row, place], axis=1),
    )


def gather_kernel(
    col_blocks,
    elig_ref,
    cnt_ref,
    row_ref,
    col_ref,
    index_out,
    tiles_out,
    lead_tiles_out,
    lead_rows_out,
    col_vmem,
    index_s,
    sem,
):
    load = pltpu.make_async_copy(col_ref, col_vmem, sem.at[0])
    load.start()
    own = lax.axis_index("camp")
    block_id, valid, lead_info = slot_index(elig_ref[...], cnt_ref[...], own, col_blocks)
    rest = jnp.zeros((5, block_id.shape[1]), jnp.int32)
    index_out[...] = jnp.concatenate([block_id, valid, lead_info, rest], axis=0)
    to_smem = pltpu.make_async_copy(index_out, index_s, sem.at[1])
    to_smem.start()
    to_smem.wait()
    load.wait()
    row_blocks = tiles_out.shape[0]

    def pick(t):
        return col_vmem[:, pl.ds(pl.multiple_of(index_s[0, t] * BLOCK, BLOCK), BLOCK)]

    def regular(b, _):
        tiles_out[b, :, 0:BLOCK] = pick(b)
        tiles_out[b, :, BLOCK : 2 * BLOCK] = pick(row_blocks + b)
        return 0

    lax.fori_loop(0, row_blocks, regular, 0, unroll=8)

    def lead(k, _):
        for s in range(LEAD_SLOTS):
            lead_tiles_out[k, :, s * BLOCK : (s + 1) * BLOCK] = pick(
                2 * row_blocks + s * LEADS + k
            )
        at = pl.multiple_of(index_s[2, k] * BLOCK, BLOCK)
        lead_rows_out[k] = row_ref[:, pl.ds(at, BLOCK)]
        return 0

    lax.fori_loop(0, LEADS, lead, 0, unroll=2)


def kernel(
    n_z,
    n_camp,
    row_ref,
    tile_ref,
    lead_tile_ref,
    lead_row_ref,
    price_ref,
    spend_ref,
    step_ref,
    idx_ref,
    out_price,
    out_norm,
    rowaug,
    leadrow,
    colaug,
    leadaug,
    sel,
    selt,
    bias,
    pg,
    pgl,
    e_ref,
    el_ref,
    m_ref,
    l_ref,
    lse_ref,
    row_in,
    norm_in,
    norm_out,
    parts,
    cols,
    sib_in,
    z_out,
    z_in,
    prices,
    row_send,
    row_recv,
    norm_send,
    norm_recv,
    sib_send,
    sib_recv,
    z_send,
    z_recv,
    pz_send,
    pz_recv,
    pc_send,
    pc_recv,
):
    dp = lax.axis_index("dp")
    camp = lax.axis_index("camp")
    z = lax.div(dp, 2)
    core = lax.rem(dp, 2)
    sibling = 2 * z + 1 - core
    row_blocks = rowaug.shape[0]
    col_blocks = price_ref.shape[0]
    half = col_blocks // 2
    chunk = half // n_z
    band = BLOCK // n_camp

    barrier = pltpu.get_barrier_semaphore()

    def greet_camp(k, _):
        peer = lax.rem(camp + k, n_camp)
        pl.semaphore_signal(barrier, inc=1, device_id=(dp, peer), device_id_type=MESH)
        return 0

    lax.fori_loop(1, n_camp, greet_camp, 0)

    def greet_z(k, _):
        peer = lax.rem(z + k, n_z)
        pl.semaphore_signal(
            barrier, inc=1, device_id=(2 * peer + core, camp), device_id_type=MESH
        )
        return 0

    lax.fori_loop(1, n_z, greet_z, 0)
    pl.semaphore_signal(barrier, inc=1, device_id=(sibling, camp), device_id_type=MESH)

    block_id = idx_ref[0:1, :]
    valid = idx_ref[1:2, :]
    wide = block_id.shape[1]
    sel[...] = jnp.where(
        (lax.broadcasted_iota(jnp.int32, (col_blocks, wide), 0) == block_id) & (valid > 0),
        1.0,
        0.0,
    ).astype(BF16)
    both = jnp.concatenate(
        [block_id.astype(F32), valid.astype(F32), jnp.zeros((6, wide), F32)], axis=0
    )
    for half_t in range(2):
        part = both[:, half_t * BLOCK : (half_t + 1) * BLOCK]
        turned = jnp.concatenate([part, jnp.zeros((BLOCK - 8, BLOCK), F32)], axis=0).T
        at = turned[:, 0:1]
        ok = turned[:, 1:2]
        lanes = lax.broadcasted_iota(jnp.int32, (BLOCK, col_blocks), 1).astype(F32)
        selt[half_t * BLOCK : (half_t + 1) * BLOCK, :] = jnp.where(
            (lanes == at) & (ok > 0.5), 1.0, 0.0
        ).astype(BF16)
        bias[half_t * BLOCK : (half_t + 1) * BLOCK, :] = jnp.broadcast_to(
            jnp.where(ok > 0.5, 0.0, DEAD), (BLOCK, BLOCK)
        )

    def widen(tile):
        scaled = tile.astype(F32) * SCALE
        hi = scaled.astype(BF16).astype(F32)
        rest = scaled - hi
        mid = rest.astype(BF16).astype(F32)
        low = rest - mid
        stack = jnp.concatenate([hi, mid, low, jnp.zeros((RANK, BLOCK), F32)], axis=0)
        return stack.T.astype(BF16)

    def make_rows(b, _):
        at = pl.multiple_of(b * BLOCK, BLOCK)
        rowaug[b] = widen(row_ref[:, pl.ds(at, BLOCK)])
        return 0

    lax.fori_loop(0, row_blocks, make_rows, 0, unroll=2)

    def thrice(tile):
        return jnp.concatenate([tile, tile, tile, jnp.zeros_like(tile)], axis=0)

    def make_cols(b, _):
        colaug[b] = thrice(tile_ref[b])
        return 0

    lax.fori_loop(0, row_blocks, make_cols, 0, unroll=4)

    def make_leads(k, _):
        leadaug[k] = thrice(lead_tile_ref[k])
        leadrow[k] = widen(lead_row_ref[k])
        return 0

    lax.fori_loop(0, LEADS, make_leads, 0)

    prices[0] = price_ref[...]
    m_ref[...] = jnp.zeros_like(m_ref)
    l_ref[...] = jnp.zeros_like(l_ref)
    parts[...] = jnp.zeros_like(parts)
    pl.semaphore_wait(barrier, (n_camp - 1) + (n_z - 1) + 1)

    lane = lax.broadcasted_iota(jnp.int32, (BLOCK, BLOCK), 1)

    def place_of(k):
        places = idx_ref[2:3, 0:BLOCK]
        at = lax.broadcasted_iota(jnp.int32, (1, BLOCK), 1) == LEADS * LEAD_SLOTS + k
        return jnp.sum(jnp.where(at, places, 0), axis=1, keepdims=True)

    def one_pass(p, _):
        scaled_price = prices[p] * SCALE
        picked = exact_pick(selt[...], scaled_price) + bias[...]
        pg[:, 0:BLOCK] = picked[0:row_blocks]
        pg[:, BLOCK : 2 * BLOCK] = picked[row_blocks : 2 * row_blocks]
        for s in range(LEAD_SLOTS):
            base = 2 * row_blocks + s * LEADS
            pgl[:, s * BLOCK : (s + 1) * BLOCK] = picked[base : base + LEADS]

        def visit(g, _):
            m_all = m_ref[...]
            l_all = l_ref[...]
            for u in range(GROUP):
                b = g * GROUP + u
                logit = mm(rowaug[b], colaug[b]) - pg[pl.ds(b, 1), :]
                top = jnp.maximum(logit[:, 0:BLOCK], logit[:, BLOCK:])
                m = jnp.maximum(jnp.max(top, axis=1, keepdims=True), 0.0)
                e = jnp.exp2(logit - m)
                e_ref[b] = e
                l = jnp.sum(e[:, 0:BLOCK] + e[:, BLOCK:], axis=1, keepdims=True)
                m_all = jnp.where(lane == b, m, m_all)
                l_all = jnp.where(lane == b, l, l_all)
            m_ref[...] = m_all
            l_ref[...] = l_all
            return 0

        lax.fori_loop(0, row_blocks // GROUP, visit, 0)

        def visit_lead(k, _):
            place = place_of(k)
            logit = mm(leadrow[k], leadaug[k]) - pgl[pl.ds(k, 1), :]
            top = logit[:, 0:BLOCK]
            for s in range(1, LEAD_SLOTS):
                top = jnp.maximum(top, logit[:, s * BLOCK : (s + 1) * BLOCK])
            m = jnp.maximum(jnp.max(top, axis=1, keepdims=True), 0.0)
            e = jnp.exp2(logit - m)
            el_ref[k] = e
            total = e[:, 0:BLOCK]
            for s in range(1, LEAD_SLOTS):
                total = total + e[:, s * BLOCK : (s + 1) * BLOCK]
            l = jnp.sum(total, axis=1, keepdims=True)
            m_ref[...] = jnp.where(lane == place, m, m_ref[...])
            l_ref[...] = jnp.where(lane == place, l, l_ref[...])
            return 0

        lax.fori_loop(0, LEADS, visit_lead, 0)

        lse_ref[p] = m_ref[...] + jnp.log2(jnp.maximum(l_ref[...], 1e-37))
        mine = pl.ds(pl.multiple_of(camp * band, band), band)

        def send_rows(k, _):
            peer = lax.rem(camp + k, n_camp)
            theirs = pl.ds(pl.multiple_of(peer * band, band), band)
            pltpu.make_async_remote_copy(
                src_ref=lse_ref.at[p, theirs],
                dst_ref=row_in.at[p, camp],
                send_sem=row_send.at[p, peer],
                recv_sem=row_recv.at[p, camp],
                device_id=(dp, peer),
                device_id_type=MESH,
            ).start()
            return 0

        lax.fori_loop(1, n_camp, send_rows, 0)
        row_in[p, camp] = lse_ref[p, mine, :]

        def wait_rows(k, _):
            peer = lax.rem(camp + k, n_camp)
            pltpu.make_async_remote_copy(
                src_ref=row_in.at[p, peer],
                dst_ref=row_in.at[p, peer],
                send_sem=row_send.at[p, peer],
                recv_sem=row_recv.at[p, peer],
                device_id=(dp, peer),
                device_id_type=MESH,
            ).wait_recv()
            return 0

        lax.fori_loop(1, n_camp, wait_rows, 0)
        every = row_in[p]
        top = jnp.maximum(jnp.max(every, axis=0), 0.0)
        total = jnp.exp2(-top) + jnp.sum(jnp.exp2(every - top[None]), axis=0)
        norm = top + jnp.log2(total)
        norm_out[p] = norm
        norm_in[p, mine, :] = norm

        def send_norm(k, _):
            peer = lax.rem(camp + k, n_camp)
            pltpu.make_async_remote_copy(
                src_ref=norm_out.at[p],
                dst_ref=norm_in.at[p, mine],
                send_sem=norm_send.at[p, peer],
                recv_sem=norm_recv.at[p, camp],
                device_id=(dp, peer),
                device_id_type=MESH,
            ).start()
            return 0

        lax.fori_loop(1, n_camp, send_norm, 0)

        def wait_norm(k, _):
            peer = lax.rem(camp + k, n_camp)
            theirs = pl.ds(pl.multiple_of(peer * band, band), band)
            pltpu.make_async_remote_copy(
                src_ref=norm_in.at[p, theirs],
                dst_ref=norm_in.at[p, theirs],
                send_sem=norm_send.at[p, peer],
                recv_sem=norm_recv.at[p, peer],
                device_id=(dp, peer),
                device_id_type=MESH,
            ).wait_recv()
            return 0

        lax.fori_loop(1, n_camp, wait_norm, 0)

        l_ref[...] = jnp.exp2(m_ref[...] - norm_in[p])

        def weigh(g, _):
            turned = pltpu.roll(l_ref[...], lax.rem(BLOCK - g * GROUP, BLOCK), 1)
            for u in range(GROUP):
                b = g * GROUP + u
                part = jnp.sum(e_ref[b] * turned[:, u : u + 1], axis=0, keepdims=True)
                parts[pl.ds(b, 1), :] = part[:, 0:BLOCK]
                parts[pl.ds(row_blocks + b, 1), :] = part[:, BLOCK:]
            return 0

        lax.fori_loop(0, row_blocks // GROUP, weigh, 0)

        def weigh_lead(k, _):
            place = place_of(k)
            w = jnp.sum(jnp.where(lane == place, l_ref[...], 0.0), axis=1, keepdims=True)
            part = jnp.sum(el_ref[k] * w, axis=0, keepdims=True)
            for s in range(LEAD_SLOTS):
                parts[pl.ds(2 * row_blocks + s * LEADS + k, 1), :] = part[
                    :, s * BLOCK : (s + 1) * BLOCK
                ]
            return 0

        lax.fori_loop(0, LEADS, weigh_lead, 0)

        cols[p] = exact_pick(sel[...], parts[...])

        def send_sib(k, _):
            peer = lax.rem(z + k, n_z)
            at = pl.multiple_of((1 - core) * half + peer * chunk, chunk)
            pltpu.make_async_remote_copy(
                src_ref=cols.at[p, pl.ds(at, chunk)],
                dst_ref=sib_in.at[p, peer],
                send_sem=sib_send.at[p, peer],
                recv_sem=sib_recv.at[p, peer],
                device_id=(sibling, camp),
                device_id_type=MESH,
            ).start()
            return 0

        lax.fori_loop(1, n_z + 1, send_sib, 0)

        def wait_sib(peer):
            pltpu.make_async_remote_copy(
                src_ref=sib_in.at[p, peer],
                dst_ref=sib_in.at[p, peer],
                send_sem=sib_send.at[p, peer],
                recv_sem=sib_recv.at[p, peer],
                device_id=(sibling, camp),
                device_id_type=MESH,
            ).wait_recv()
            at = pl.multiple_of(core * half + peer * chunk, chunk)
            return cols[p, pl.ds(at, chunk), :] + sib_in[p, peer]

        def send_z(k, _):
            peer = lax.rem(z + k, n_z)
            z_out[p, peer] = wait_sib(peer)
            pltpu.make_async_remote_copy(
                src_ref=z_out.at[p, peer],
                dst_ref=z_in.at[p, z],
                send_sem=z_send.at[p, peer],
                recv_sem=z_recv.at[p, z],
                device_id=(2 * peer + core, camp),
                device_id_type=MESH,
            ).start()
            return 0

        lax.fori_loop(1, n_z, send_z, 0)
        total = wait_sib(z)

        def wait_z(k, total):
            peer = lax.rem(z + k, n_z)
            pltpu.make_async_remote_copy(
                src_ref=z_in.at[p, peer],
                dst_ref=z_in.at[p, peer],
                send_sem=z_send.at[p, peer],
                recv_sem=z_recv.at[p, peer],
                device_id=(2 * peer + core, camp),
                device_id_type=MESH,
            ).wait_recv()
            return total + z_in[p, peer]

        total = lax.fori_loop(1, n_z, wait_z, total)
        here = pl.ds(pl.multiple_of(core * half + z * chunk, chunk), chunk)
        prices[p + 1, here, :] = jnp.maximum(
            prices[p, here, :] + step_ref[p] * (total - spend_ref[here, :]), 0.0
        )

        def send_price(k, _):
            peer = lax.rem(z + k, n_z)
            pltpu.make_async_remote_copy(
                src_ref=prices.at[p + 1, here],
                dst_ref=prices.at[p + 1, here],
                send_sem=pz_send.at[p, peer],
                recv_sem=pz_recv.at[p, z],
                device_id=(2 * peer + core, camp),
                device_id_type=MESH,
            ).start()
            return 0

        lax.fori_loop(1, n_z, send_price, 0)

        def pass_on(peer):
            at = pl.ds(pl.multiple_of(core * half + peer * chunk, chunk), chunk)
            pltpu.make_async_remote_copy(
                src_ref=prices.at[p + 1, at],
                dst_ref=prices.at[p + 1, at],
                send_sem=pc_send.at[p, peer],
                recv_sem=pc_recv.at[p, peer],
                device_id=(sibling, camp),
                device_id_type=MESH,
            ).start()

        pass_on(z)

        def forward(k, _):
            peer = lax.rem(z + k, n_z)
            at = pl.ds(pl.multiple_of(core * half + peer * chunk, chunk), chunk)
            pltpu.make_async_remote_copy(
                src_ref=prices.at[p + 1, at],
                dst_ref=prices.at[p + 1, at],
                send_sem=pz_send.at[p, peer],
                recv_sem=pz_recv.at[p, peer],
                device_id=(2 * peer + core, camp),
                device_id_type=MESH,
            ).wait_recv()
            pass_on(peer)
            return 0

        lax.fori_loop(1, n_z, forward, 0)

        def wait_price(peer, _):
            at = pl.ds(pl.multiple_of((1 - core) * half + peer * chunk, chunk), chunk)
            pltpu.make_async_remote_copy(
                src_ref=prices.at[p + 1, at],
                dst_ref=prices.at[p + 1, at],
                send_sem=pc_send.at[p, peer],
                recv_sem=pc_recv.at[p, peer],
                device_id=(sibling, camp),
                device_id_type=MESH,
            ).wait_recv()
            return 0

        lax.fori_loop(0, n_z, wait_price, 0)
        return 0

    lax.fori_loop(0, PASSES, one_pass, 0)
    out_price[...] = prices[PASSES]
    out_norm[...] = (norm_in[PASSES - 1] * LN2).T[0:row_blocks, :]

    def drain(p, _):
        def drain_camp(k, _):
            peer = lax.rem(camp + k, n_camp)
            for src, sem in ((row_in, row_send), (row_in, norm_send)):
                pltpu.make_async_remote_copy(
                    src_ref=src.at[p, peer],
                    dst_ref=src.at[p, peer],
                    send_sem=sem.at[p, peer],
                    recv_sem=row_recv.at[p, peer],
                    device_id=(dp, peer),
                    device_id_type=MESH,
                ).wait_send()
            return 0

        lax.fori_loop(1, n_camp, drain_camp, 0)

        def drain_chunk(sem, peer):
            pltpu.make_async_remote_copy(
                src_ref=z_in.at[p, peer],
                dst_ref=z_in.at[p, peer],
                send_sem=sem.at[p, peer],
                recv_sem=z_recv.at[p, peer],
                device_id=(sibling, camp),
                device_id_type=MESH,
            ).wait_send()

        def drain_z(k, _):
            peer = lax.rem(z + k, n_z)
            drain_chunk(z_send, peer)
            drain_chunk(pz_send, peer)
            return 0

        lax.fori_loop(1, n_z, drain_z, 0)

        def drain_sib(peer, _):
            drain_chunk(sib_send, peer)
            drain_chunk(pc_send, peer)
            return 0

        lax.fori_loop(0, n_z, drain_sib, 0)
        return 0

    lax.fori_loop(0, PASSES, drain, 0)


def local(
    n_dp, n_camp, row_factors, col_factors, prices, spend_target, step_sizes, eligible, counts
):
    row_blocks, slots = eligible.shape
    col_blocks = prices.shape[0] // BLOCK
    n_z = n_dp // 2
    band = BLOCK // n_camp
    chunk = col_blocks // 2 // n_z
    wide = 256
    dma = pltpu.SemaphoreType.DMA
    vmem = pltpu.VMEM
    spec = pl.BlockSpec(memory_space=pltpu.VMEM)
    rows_t = row_factors.T
    smem = pl.BlockSpec(memory_space=pltpu.SMEM)
    index, tiles, lead_tiles, lead_rows = pl.pallas_call(
        functools.partial(gather_kernel, col_blocks),
        out_shape=(
            jax.ShapeDtypeStruct((8, wide), jnp.int32),
            jax.ShapeDtypeStruct((row_blocks, RANK, 2 * BLOCK), BF16),
            jax.ShapeDtypeStruct((LEADS, RANK, LEAD_SLOTS * BLOCK), BF16),
            jax.ShapeDtypeStruct((LEADS, RANK, BLOCK), BF16),
        ),
        in_specs=[spec, spec, spec, pl.BlockSpec(memory_space=pl.ANY)],
        out_specs=(spec,) * 4,
        scratch_shapes=[
            vmem((RANK, col_blocks * BLOCK), BF16),
            pltpu.SMEM((8, wide), jnp.int32),
            dma((2,)),
        ],
        compiler_params=pltpu.CompilerParams(vmem_limit_bytes=24 * 1024 * 1024),
    )(eligible.T, counts.reshape(1, row_blocks), rows_t, col_factors.T)
    new_prices, norms = pl.pallas_call(
        functools.partial(kernel, n_z, n_camp),
        out_shape=(
            jax.ShapeDtypeStruct((col_blocks, BLOCK), F32),
            jax.ShapeDtypeStruct((row_blocks, BLOCK), F32),
        ),
        in_specs=[spec] * 6 + [smem, spec],
        out_specs=(spec, spec),
        scratch_shapes=[
            vmem((row_blocks, BLOCK, BLOCK), BF16),
            vmem((LEADS, BLOCK, BLOCK), BF16),
            vmem((row_blocks, BLOCK, 2 * BLOCK), BF16),
            vmem((LEADS, BLOCK, LEAD_SLOTS * BLOCK), BF16),
            vmem((col_blocks, wide), BF16),
            vmem((wide, col_blocks), BF16),
            vmem((wide, BLOCK), F32),
            vmem((row_blocks, 2 * BLOCK), F32),
            vmem((LEADS, LEAD_SLOTS * BLOCK), F32),
            vmem((row_blocks, BLOCK, 2 * BLOCK), F32),
            vmem((LEADS, BLOCK, LEAD_SLOTS * BLOCK), F32),
            vmem((BLOCK, BLOCK), F32),
            vmem((BLOCK, BLOCK), F32),
            vmem((PASSES, BLOCK, BLOCK), F32),
            vmem((PASSES, n_camp, band, BLOCK), F32),
            vmem((PASSES, BLOCK, BLOCK), F32),
            vmem((PASSES, band, BLOCK), F32),
            vmem((wide, BLOCK), F32),
            vmem((PASSES, col_blocks, BLOCK), F32),
            vmem((PASSES, n_z, chunk, BLOCK), F32),
            vmem((PASSES, n_z, chunk, BLOCK), F32),
            vmem((PASSES, n_z, chunk, BLOCK), F32),
            vmem((PASSES + 1, col_blocks, BLOCK), F32),
            dma((PASSES, n_camp)),
            dma((PASSES, n_camp)),
            dma((PASSES, n_camp)),
            dma((PASSES, n_camp)),
            dma((PASSES, n_z)),
            dma((PASSES, n_z)),
            dma((PASSES, n_z)),
            dma((PASSES, n_z)),
            dma((PASSES, n_z)),
            dma((PASSES, n_z)),
            dma((PASSES, n_z)),
            dma((PASSES, n_z)),
        ],
        compiler_params=pltpu.CompilerParams(
            collective_id=0, has_side_effects=True, vmem_limit_bytes=40 * 1024 * 1024
        ),
    )(
        rows_t,
        tiles,
        lead_tiles,
        lead_rows,
        prices.reshape(col_blocks, BLOCK),
        spend_target.reshape(col_blocks, BLOCK),
        step_sizes,
        index,
    )
    return new_prices.reshape(-1), norms.reshape(-1)


def solution(mesh):
    placed = (P("dp", None), P("camp", None), P("camp"), P("camp"), P(), P("dp", None), P("dp"))
    return jax.shard_map(
        functools.partial(local, mesh.shape["dp"], mesh.shape["camp"]),
        mesh=mesh,
        in_specs=placed,
        out_specs=(P("camp"), P("dp")),
        check_vma=False,
    )
```

time: 893 us -> 142 us (0.16)
  waiting for transfers between devices: 398 us -> 0 us
  blocking collectives: 349 us -> 0 us
  Pallas kernels: 0 us -> 136 us
  other arithmetic: 88.5 us -> 0 us
  local copies, waits for them, and re-layouts: 27.4 us -> 5.95 us
  matrix products: 14.5 us -> 0 us
  between operations: 14.3 us -> 0.7 us
    psum x3 -> x0, waiting for transfers between devices: 398 us -> none  [local(): colsum = lax.psum(local_cols, 'dp')]
    pmax x3 -> x0, blocking collectives: 181 us -> none  [row_normalizer(): top_value = lax.pmax(local_top, 'camp')]
    psum x3 -> x0, blocking collectives: 168 us -> none  [row_normalizer(): sum_value = lax.psum(local_sum, 'camp')]
    pallas_call x0 -> x2, Pallas kernels: none -> 136 us  [the longest x1 134 us: local(): pl.pallas_call(functools.partial(kernel, n_z, n_camp), out_shape=(jax.Sha...]
    reduce_sum x12 -> x0, other arithmetic: 55.2 us -> none  [the longest x6 21.5 us: masked_sum(): jnp.sum(jnp.where(live_mask, jnp.exp(logit_values - top_value[:, None, :,...]
    gather x27 -> x0, local copies, waits for them, and re-layouts: 19.8 us -> none  [the longest x8 3.29 us: slot_tiles(): chosen = jnp.take_along_axis(slot_ids, picked, axis=1)]
    reduce_max x4 -> x0, other arithmetic: 16.5 us -> none  [the longest x2 10.7 us: row_normalizer(): jnp.max(jnp.where(mask_all, every_logit, -jnp.inf), axis=(1, 3))]
    dot_general x8 -> x0, matrix products: 14.5 us -> none  [the longest x1 6.23 us: local(): jnp.einsum('brk,bmck->bmrc', row_tiles, col_tiles[every_block], preferred...]
  transfers between devices with their start and end apart: 3 -> 0, of which waited for: 3 -> 0; matrix products, arithmetic and copies ran while one was open for 0% -> 0% of each run, Pallas kernels for 0% -> 0%
where the time goes in v1:
time: 142 us
  Pallas kernels  136 us (96%)
  local copies, waits for them, and re-layouts  5.95 us (4%)
    pallas_call x1, Pallas kernels, local(): pl.pallas_call(functools.partial(kernel, n_z, n_camp), out_shape=(jax.Sha...  134 us
    unnamed x18, local copies, waits for them, and re-layouts  5.95 us

profile of v1, /device:TPU:1, one launch (start us, length us, event | category | flops | bytes accessed | tf_op | source)
XLA Modules:
  0.0 142.2 jit_solution(731223430003322664)
XLA Ops:
  0.6 0.0 copy-start.7
  0.6 0.0 copy-start
  0.7 2.2 %copy-done = bf16[65536,32]{0,1:T(8,128)(2,1)S(1)} copy-done((bf16[65536,32]{0,1:T(8,128)(2,1)S(1)}, bf16[65536,32]{0,1:T(8,128)(2,1)}, u32[]{:S(2)}) %copy-start) | copy-done | bytes 4194328
  2.8 0.0 copy-start.1
  2.8 1.0 copy-done.1
  3.9 0.0 copy-start.5
  3.9 0.7 copy-done.5
  4.6 0.0 copy-start.6
  4.6 0.7 copy-done.6
  5.3 0.0 copy-start.2
  5.3 0.0 copy-start.3
  5.3 0.0 copy-start.4
  5.3 1.9 %shard_map.86 = (s32[8,256]{1,0:T(8,128)S(1)}, bf16[64,32,256]{2,1,0:T(8,128)(2,1)S(1)}, bf16[8,32,1024]{2,1,0:T(8,128)(2,1)S(1)}, bf16[8,32,128]{2,1,0:T(8,128)(2,1)S(1)}) custom-call(s32[32,64]{1,0:T(8,128)S(1)} %bitcast.15, s32[1,64]{1,0:T(1,128)S(1)} %bitcast.16, bf16[32,8192]{1,0:T(8,128)(2,1)S(1)} %bitcast.9, bf16[32,65536]{1,0:T(8,128)(2,1)S(1)} %bitcast.8), custom_call_target="tpu_custom_call" | custom-call | tf_op jit(solution)/shard_map/pallas_call | solution.py:632
  7.2 0.0 copy-done.7
  7.2 0.0 copy-done.2
  7.2 0.0 copy-done.3
  7.2 0.0 copy-done.4
  7.2 133.7 %shard_map.87 = (f32[512,128]{1,0:T(8,128)S(1)}, f32[64,128]{1,0:T(8,128)S(1)}) custom-call(bf16[32,8192]{1,0:T(8,128)(2,1)S(1)} %bitcast.10, bf16[64,32,256]{2,1,0:T(8,128)(2,1)S(1)} %get-tuple-element.8.tile_ref, bf16[8,32,1024]{2,1,0:T(8,128)(2,1)S(1)} %get-tuple-element.9.lead_tile_ref, bf16[8,32,128]{2,1,0:T(8,128)(2,1)S(1)} %get-tuple-element.10.lead_row_ref, ...), custom_call_target="tpu_custom_call" | custom-call | tf_op jit(solution)/shard_map/pallas_call | solution.py:649
  140.9 0.7 copy.11
  141.6 0.6 copy.12
Async XLA Ops:
  0.6 6.6 %copy-start.7 = (f32[3]{0:T(128)S(1)}, f32[3]{0:T(128)}, u32[]{:S(2)}) copy-start(f32[3]{0:T(128)} %step_ref.1) | copy-start | bytes 40
  0.6 2.2 %copy-start = (bf16[65536,32]{0,1:T(8,128)(2,1)S(1)}, bf16[65536,32]{0,1:T(8,128)(2,1)}, u32[]{:S(2)}) copy-start(bf16[65536,32]{0,1:T(8,128)(2,1)} %param.8) | copy-start | bytes 12582916
  2.8 1.0 copy-start.1
  3.9 0.7 copy-start.5
  4.6 0.7 copy-start.6
  5.3 1.9 %copy-start.2 = (bf16[8192,32]{0,1:T(8,128)(2,1)S(1)}, bf16[8192,32]{0,1:T(8,128)(2,1)}, u32[]{:S(2)}) copy-start(bf16[8192,32]{0,1:T(8,128)(2,1)} %param.7) | copy-start | bytes 1572868
  5.3 1.9 %copy-start.3 = (f32[65536]{0:T(1024)S(1)}, f32[65536]{0:T(1024)}, u32[]{:S(2)}) copy-start(f32[65536]{0:T(1024)} %param.9) | copy-start | bytes 786436
  5.3 2.0 %copy-start.4 = (f32[65536]{0:T(1024)S(1)}, f32[65536]{0:T(1024)}, u32[]{:S(2)}) copy-start(f32[65536]{0:T(1024)} %param.10) | copy-start | bytes 786436

commit v2 on v1

v2 whole, which is shorter than its diff:
```python
import functools
import math

import jax
import jax.numpy as jnp
from jax import lax
from jax.experimental import pallas as pl
from jax.experimental.pallas import tpu as pltpu
from jax.sharding import PartitionSpec as P

MESH = pl.DeviceIdType.MESH
F32 = jnp.float32
BF16 = jnp.bfloat16
BLOCK = 128
RANK = 32
PASSES = 3
LEADS = 8
LEAD_SLOTS = 8
SCALE = math.log2(math.e) / 0.3
LN2 = math.log(2.0)
DEAD = 1e30
CHUNK = 16


def pieces(x):
    hi = x.astype(BF16)
    rest = x - hi.astype(F32)
    mid = rest.astype(BF16)
    low = (rest - mid.astype(F32)).astype(BF16)
    return hi, mid, low


def mm(a, b):
    return lax.dot_general(a, b, (((1,), (0,)), ((), ())), preferred_element_type=F32)


def mm_tn(a, b):
    return lax.dot_general(a, b, (((0,), (0,)), ((), ())), preferred_element_type=F32)


def mm_nt(a, b):
    return lax.dot_general(a, b, (((1,), (1,)), ((), ())), preferred_element_type=F32)


def exact_pick(select, x):
    hi, mid, low = pieces(x)
    out = mm(select, jnp.concatenate([hi, mid, low], axis=1))
    return out[:, :BLOCK] + out[:, BLOCK : 2 * BLOCK] + out[:, 2 * BLOCK :]


def slot_index(elig, cnt, own, col_blocks):
    slots, rows = elig.shape
    pos = lax.broadcasted_iota(jnp.int32, elig.shape, 0)
    owned = lax.div(elig, col_blocks) == own
    led = owned[0:1, :]
    first = jnp.min(jnp.where(owned, pos, slots), axis=0, keepdims=True)
    blocks, valids = [], []
    for k in range(2):
        picked = first + k
        chosen = jnp.sum(jnp.where(pos == picked, elig, 0), axis=0, keepdims=True)
        ok = (
            (picked < slots)
            & (lax.div(chosen, col_blocks) == own)
            & (picked < cnt)
            & jnp.logical_not(led)
        )
        blocks.append(jnp.where(ok, chosen - own * col_blocks, 0))
        valids.append(ok.astype(jnp.int32))
    led_f = jnp.broadcast_to(led.astype(F32), (8, rows))
    before = (
        lax.broadcasted_iota(jnp.int32, (rows, rows), 0)
        < lax.broadcasted_iota(jnp.int32, (rows, rows), 1)
    ).astype(F32)
    rank = mm(led_f.astype(BF16), before.astype(BF16))[0:1, :]
    lane = lax.broadcasted_iota(jnp.int32, (LEADS * LEAD_SLOTS, rows), 0)
    hot = jnp.where((rank == lax.rem(lane, LEADS).astype(F32)) & led, 1.0, 0.0)
    row_id = lax.broadcasted_iota(jnp.int32, (8, rows), 1).astype(F32)
    high = lax.div(elig, 128)
    picked = mm_nt(
        jnp.concatenate(
            [
                high.astype(F32),
                (elig - high * 128).astype(F32),
                jnp.broadcast_to(cnt, (8, rows)).astype(F32),
                jnp.ones((8, rows), F32),
                row_id,
            ],
            axis=0,
        ).astype(BF16),
        hot.astype(BF16),
    )
    wide = LEADS * LEAD_SLOTS
    every = picked[0:slots] * 128.0 + picked[slots : 2 * slots]
    slot_of = lax.div(lax.broadcasted_iota(jnp.int32, (slots, wide), 1), LEADS)
    chosen = jnp.sum(
        jnp.where(lax.broadcasted_iota(jnp.int32, (slots, wide), 0) == slot_of, every, 0.0),
        axis=0,
        keepdims=True,
    ).astype(jnp.int32)
    lead_cnt = picked[2 * slots : 2 * slots + 1]
    exists = picked[2 * slots + 8 : 2 * slots + 9] > 0.5
    lead_row = picked[2 * slots + 16 : 2 * slots + 17].astype(jnp.int32)
    ok = exists & (slot_of[0:1].astype(F32) < lead_cnt)
    blocks.append(jnp.where(ok, chosen - own * col_blocks, 0))
    valids.append(ok.astype(jnp.int32))
    blocks.append(jnp.zeros_like(lead_row))
    valids.append(jnp.zeros_like(lead_row))
    place = jnp.where(exists, lead_row, -1)
    return (
        jnp.concatenate(blocks, axis=1),
        jnp.concatenate(valids, axis=1),
        jnp.concatenate([lead_row, place, lead_row, place], axis=1),
    )


def gather_kernel(
    col_blocks,
    elig_hbm,
    cnt_hbm,
    row_hbm,
    col_hbm,
    index_out,
    tiles_out,
    lead_tiles_out,
    lead_rows_out,
    elig_ref,
    cnt_ref,
    row_ref,
    col_ref,
    index_s,
    sem,
):
    loads = [
        pltpu.make_async_copy(src, dst, sem.at[i])
        for i, (src, dst) in enumerate(
            ((elig_hbm, elig_ref), (cnt_hbm, cnt_ref), (col_hbm, col_ref), (row_hbm, row_ref))
        )
    ]
    for load in loads:
        load.start()
    own = lax.axis_index("camp")
    loads[0].wait()
    loads[1].wait()
    block_id, valid, lead_info = slot_index(elig_ref[...], cnt_ref[...], own, col_blocks)
    rest = jnp.zeros((5, block_id.shape[1]), jnp.int32)
    index_out[...] = jnp.concatenate([block_id, valid, lead_info, rest], axis=0)
    to_smem = pltpu.make_async_copy(index_out, index_s, sem.at[4])
    to_smem.start()
    to_smem.wait()
    loads[2].wait()
    row_blocks = tiles_out.shape[0]

    def pick(t):
        return col_ref[:, pl.ds(pl.multiple_of(index_s[0, t] * BLOCK, BLOCK), BLOCK)]

    def regular(b, _):
        tiles_out[b, :, 0:BLOCK] = pick(b)
        tiles_out[b, :, BLOCK : 2 * BLOCK] = pick(row_blocks + b)
        return 0

    lax.fori_loop(0, row_blocks, regular, 0, unroll=8)
    loads[3].wait()

    def lead(k, _):
        for s in range(LEAD_SLOTS):
            lead_tiles_out[k, :, s * BLOCK : (s + 1) * BLOCK] = pick(
                2 * row_blocks + s * LEADS + k
            )
        at = pl.multiple_of(index_s[2, k] * BLOCK, BLOCK)
        lead_rows_out[k] = row_ref[:, pl.ds(at, BLOCK)]
        return 0

    lax.fori_loop(0, LEADS, lead, 0, unroll=2)


def far_first(side):
    return sorted(range(1, side), key=lambda k: -min(k, side - k))


def kernel(
    n_z,
    side,
    row_hbm,
    tile_hbm,
    lead_tile_hbm,
    lead_row_hbm,
    price_hbm,
    spend_hbm,
    step_ref,
    idx_hbm,
    out_price,
    out_norm,
    row_ref,
    tile_ref,
    lead_tile_ref,
    lead_row_ref,
    spend_ref,
    idx_ref,
    sel,
    selt,
    bias,
    pg,
    pgl,
    s_ref,
    sl_ref,
    e_ref,
    el_ref,
    sum_ref,
    lead_sum_ref,
    m_ref,
    l_ref,
    ml_ref,
    ll_ref,
    turn_ref,
    lse_ref,
    row_in,
    parts,
    cols,
    sib_in,
    z_out,
    z_in,
    prices,
    load_sem,
    row_send,
    row_recv,
    sib_send,
    sib_recv,
    z_send,
    z_recv,
    pz_send,
    pz_recv,
    pc_send,
    pc_recv,
):
    dp = lax.axis_index("dp")
    camp = lax.axis_index("camp")
    z = lax.div(dp, 2)
    core = lax.rem(dp, 2)
    x = lax.div(camp, side)
    y = lax.rem(camp, side)
    sibling = 2 * z + 1 - core
    row_blocks = s_ref.shape[0]
    chunks = row_blocks // CHUNK
    col_blocks = spend_ref.shape[0]
    half = col_blocks // 2
    chunk = half // n_z
    n_camp = side * side

    loads = [
        pltpu.make_async_copy(src, dst, load_sem.at[i])
        for i, (src, dst) in enumerate(
            (
                (idx_hbm, idx_ref),
                (price_hbm, prices.at[0]),
                (row_hbm, row_ref),
                (tile_hbm, tile_ref),
                (lead_row_hbm, lead_row_ref),
                (lead_tile_hbm, lead_tile_ref),
                (spend_hbm, spend_ref),
            )
        )
    ]
    for load in loads:
        load.start()

    hops = [min(k, side - k) for k in range(side)]
    camp_peers = [
        lax.rem(x + dx, side) * side + lax.rem(y + dy, side)
        for dx, dy in sorted(
            ((a, b) for a in range(side) for b in range(side) if a or b),
            key=lambda ab: -hops[ab[0]] - hops[ab[1]],
        )
    ]
    z_peers = [lax.rem(z + k, n_z) for k in far_first(n_z)]

    barrier = pltpu.get_barrier_semaphore()
    for peer in camp_peers:
        pl.semaphore_signal(barrier, inc=1, device_id=(dp, peer), device_id_type=MESH)
    for peer in z_peers:
        pl.semaphore_signal(
            barrier, inc=1, device_id=(2 * peer + core, camp), device_id_type=MESH
        )
    pl.semaphore_signal(barrier, inc=1, device_id=(sibling, camp), device_id_type=MESH)

    loads[0].wait()
    block_id = idx_ref[0:1, :]
    valid = idx_ref[1:2, :]
    wide = block_id.shape[1]
    both = jnp.concatenate(
        [block_id.astype(F32), valid.astype(F32), jnp.zeros((6, wide), F32)], axis=0
    )
    for half_t in range(2):
        part = both[:, half_t * BLOCK : (half_t + 1) * BLOCK]
        turned = jnp.concatenate([part, jnp.zeros((BLOCK - 8, BLOCK), F32)], axis=0).T
        at = turned[:, 0:1]
        ok = turned[:, 1:2]
        lanes = lax.broadcasted_iota(jnp.int32, (BLOCK, col_blocks), 1).astype(F32)
        selt[half_t * BLOCK : (half_t + 1) * BLOCK, :] = jnp.where(
            (lanes == at) & (ok > 0.5), 1.0, 0.0
        ).astype(BF16)
        bias[half_t * BLOCK : (half_t + 1) * BLOCK, :] = jnp.broadcast_to(
            jnp.where(ok > 0.5, 0.0, DEAD), (BLOCK, BLOCK)
        )

    loads[2].wait()
    loads[3].wait()

    def score(b, _):
        at = pl.multiple_of(b * BLOCK, BLOCK)
        s_ref[b] = mm_tn(row_ref[:, pl.ds(at, BLOCK)], tile_ref[b]) * SCALE
        return 0

    lax.fori_loop(0, row_blocks, score, 0, unroll=8)
    loads[4].wait()
    loads[5].wait()

    def score_lead(k, _):
        sl_ref[k] = mm_tn(lead_row_ref[k], lead_tile_ref[k]) * SCALE
        return 0

    lax.fori_loop(0, LEADS, score_lead, 0, unroll=2)

    parts[...] = jnp.zeros_like(parts)
    turn_ref[...] = jnp.zeros_like(turn_ref)
    loads[1].wait()
    loads[6].wait()
    pl.semaphore_wait(barrier, (n_camp - 1) + (n_z - 1) + 1)

    lane = lax.broadcasted_iota(jnp.int32, (BLOCK, BLOCK), 1)

    def place_of(k):
        places = idx_ref[2:3, 0:BLOCK]
        at = lax.broadcasted_iota(jnp.int32, (1, BLOCK), 1) == LEADS * LEAD_SLOTS + k
        return jnp.sum(jnp.where(at, places, 0), axis=1, keepdims=True)

    def price_rows(of_core, peer):
        return pl.ds(pl.multiple_of(of_core * half + peer * chunk, chunk), chunk)

    def row_copy(p, c, src, dst, peer, slot):
        rows = pl.ds(pl.multiple_of(c * CHUNK, CHUNK), CHUNK)
        return pltpu.make_async_remote_copy(
            src_ref=src.at[p, rows],
            dst_ref=dst.at[p, slot, rows],
            send_sem=row_send.at[p, c, peer],
            recv_sem=row_recv.at[p, c, slot],
            device_id=(dp, peer),
            device_id_type=MESH,
        )

    def sib_copy(p, peer):
        return pltpu.make_async_remote_copy(
            src_ref=cols.at[p, price_rows(1 - core, peer)],
            dst_ref=sib_in.at[p, peer],
            send_sem=sib_send.at[p, peer],
            recv_sem=sib_recv.at[p, peer],
            device_id=(sibling, camp),
            device_id_type=MESH,
        )

    def z_copy(p, peer, slot):
        return pltpu.make_async_remote_copy(
            src_ref=z_out.at[p, peer],
            dst_ref=z_in.at[p, slot],
            send_sem=z_send.at[p, peer],
            recv_sem=z_recv.at[p, slot],
            device_id=(2 * peer + core, camp),
            device_id_type=MESH,
        )

    def price_copy(p, peer, owner):
        rows = price_rows(core, owner)
        return pltpu.make_async_remote_copy(
            src_ref=prices.at[p + 1, rows],
            dst_ref=prices.at[p + 1, rows],
            send_sem=pz_send.at[p, peer],
            recv_sem=pz_recv.at[p, owner],
            device_id=(2 * peer + core, camp),
            device_id_type=MESH,
        )

    def cross_copy(p, of_core, owner):
        rows = price_rows(of_core, owner)
        return pltpu.make_async_remote_copy(
            src_ref=prices.at[p + 1, rows],
            dst_ref=prices.at[p + 1, rows],
            send_sem=pc_send.at[p, owner],
            recv_sem=pc_recv.at[p, owner],
            device_id=(sibling, camp),
            device_id_type=MESH,
        )

    def one_pass(p, _):
        picked = exact_pick(selt[...], prices[p] * SCALE) + bias[...]
        pg[:, 0:BLOCK] = picked[0:row_blocks]
        pg[:, BLOCK : 2 * BLOCK] = picked[row_blocks : 2 * row_blocks]
        for s in range(LEAD_SLOTS):
            base = 2 * row_blocks + s * LEADS
            pgl[:, s * BLOCK : (s + 1) * BLOCK] = picked[base : base + LEADS]
        ml_ref[...] = jnp.zeros_like(ml_ref)
        ll_ref[...] = jnp.zeros_like(ll_ref)

        def visit_lead(k, _):
            place = place_of(k)
            price = pgl[pl.ds(k, 1), :]
            for r in range(0, BLOCK, 32):
                logit = sl_ref[k, r : r + 32, :] - price
                top = logit[:, 0:BLOCK]
                for s in range(1, LEAD_SLOTS):
                    top = jnp.maximum(top, logit[:, s * BLOCK : (s + 1) * BLOCK])
                m = jnp.maximum(jnp.max(top, axis=1, keepdims=True), 0.0)
                e = jnp.exp2(logit - m)
                el_ref[k, r : r + 32, :] = e
                total = e[:, 0:BLOCK]
                for s in range(1, LEAD_SLOTS):
                    total = total + e[:, s * BLOCK : (s + 1) * BLOCK]
                lead_sum_ref[k, r : r + 32, :] = total
                ml_ref[r : r + 32, :] = jnp.where(
                    lane[r : r + 32] == place, m, ml_ref[r : r + 32, :]
                )
            return 0

        lax.fori_loop(0, LEADS, visit_lead, 0, unroll=2)

        def add_lead(k, _):
            place = place_of(k)
            l = jnp.sum(lead_sum_ref[k], axis=1, keepdims=True)
            ll_ref[...] = jnp.where(lane == place, l, ll_ref[...])
            return 0

        lax.fori_loop(0, LEADS, add_lead, 0, unroll=8)
        m_ref[...] = ml_ref[...]

        def visit(c, _):
            m_all = jnp.zeros((BLOCK, BLOCK), F32)
            for u in range(CHUNK):
                b = c * CHUNK + u
                logit = s_ref[b] - pg[pl.ds(b, 1), :]
                top = jnp.maximum(logit[:, 0:BLOCK], logit[:, BLOCK:])
                m = jnp.maximum(jnp.max(top, axis=1, keepdims=True), 0.0)
                e = jnp.exp2(logit - m)
                e_ref[b] = e
                sum_ref[u] = e[:, 0:BLOCK] + e[:, BLOCK:]
                m_all = jnp.where(lane == b, m, m_all)
            m_ref[...] = m_ref[...] + m_all
            l_all = ll_ref[...]
            for u in range(CHUNK):
                l = jnp.sum(sum_ref[u], axis=1, keepdims=True)
                l_all = l_all + jnp.where(lane == c * CHUNK + u, l, 0.0)
            l_ref[...] = (m_ref[...] + jnp.log2(jnp.maximum(l_all, 1e-37))).T
            rows = pl.ds(pl.multiple_of(c * CHUNK, CHUNK), CHUNK)
            lse = l_ref[rows, :]
            lse_ref[p, rows, :] = lse
            row_in[p, camp, rows, :] = lse
            for peer in camp_peers:
                row_copy(p, c, lse_ref, row_in, peer, camp).start()
            return 0

        lax.fori_loop(0, chunks, visit, 0)

        @pl.when(p == 0)
        def _():
            sel[...] = jnp.where(
                (lax.broadcasted_iota(jnp.int32, (col_blocks, wide), 0) == block_id)
                & (valid > 0),
                1.0,
                0.0,
            ).astype(BF16)

        def weigh(c, _):
            rows = pl.ds(pl.multiple_of(c * CHUNK, CHUNK), CHUNK)
            for peer in camp_peers[::-1]:
                row_copy(p, c, lse_ref, row_in, peer, peer).wait_recv()
            every = row_in[p, :, rows, :]
            top = jnp.maximum(jnp.max(every, axis=0), 0.0)
            total = jnp.exp2(-top) + jnp.sum(jnp.exp2(every - top[None]), axis=0)
            turn_ref[rows, :] = top + jnp.log2(total)
            weight = jnp.exp2(m_ref[...] - turn_ref[...].T)
            l_ref[...] = weight
            turned = pltpu.roll(weight, lax.rem(BLOCK - c * CHUNK, BLOCK), 1)
            first, second = [], []
            for u in range(CHUNK):
                part = jnp.sum(
                    e_ref[c * CHUNK + u] * turned[:, u : u + 1], axis=0, keepdims=True
                )
                first.append(part[:, 0:BLOCK])
                second.append(part[:, BLOCK:])
            parts[rows, :] = jnp.concatenate(first, axis=0)
            parts[pl.ds(pl.multiple_of(row_blocks + c * CHUNK, CHUNK), CHUNK), :] = (
                jnp.concatenate(second, axis=0)
            )
            return 0

        lax.fori_loop(0, chunks, weigh, 0)

        def weigh_lead(k, _):
            place = place_of(k)
            w = jnp.sum(jnp.where(lane == place, l_ref[...], 0.0), axis=1, keepdims=True)
            part = jnp.sum(el_ref[k] * w, axis=0, keepdims=True)
            for s in range(LEAD_SLOTS):
                parts[pl.ds(2 * row_blocks + s * LEADS + k, 1), :] = part[
                    :, s * BLOCK : (s + 1) * BLOCK
                ]
            return 0

        lax.fori_loop(0, LEADS, weigh_lead, 0, unroll=4)

        cols[p] = exact_pick(sel[...], parts[...])
        for peer in z_peers:
            sib_copy(p, peer).start()
        sib_copy(p, z).start()
        for peer in z_peers:
            sib_copy(p, peer).wait_recv()
            z_out[p, peer] = cols[p, price_rows(core, peer), :] + sib_in[p, peer]
            z_copy(p, peer, z).start()
        sib_copy(p, z).wait_recv()
        here = price_rows(core, z)
        total = cols[p, here, :] + sib_in[p, z]
        for peer in z_peers[::-1]:
            z_copy(p, peer, peer).wait_recv()
            total = total + z_in[p, peer]
        prices[p + 1, here, :] = jnp.maximum(
            prices[p, here, :] + step_ref[p] * (total - spend_ref[here, :]), 0.0
        )
        for peer in z_peers:
            price_copy(p, peer, z).start()
        cross_copy(p, core, z).start()
        for peer in z_peers[::-1]:
            price_copy(p, peer, peer).wait_recv()
            cross_copy(p, core, peer).start()
        cross_copy(p, 1 - core, z).wait_recv()
        for peer in z_peers[::-1]:
            cross_copy(p, 1 - core, peer).wait_recv()
        return 0

    lax.fori_loop(0, PASSES, one_pass, 0)
    out_price[...] = prices[PASSES]
    out_norm[...] = turn_ref[0:row_blocks, :] * LN2

    def drain(p, _):
        def drain_rows(c, _):
            for peer in camp_peers:
                row_copy(p, c, lse_ref, row_in, peer, camp).wait_send()
            return 0

        lax.fori_loop(0, chunks, drain_rows, 0)
        for peer in z_peers:
            sib_copy(p, peer).wait_send()
            z_copy(p, peer, z).wait_send()
            price_copy(p, peer, z).wait_send()
            cross_copy(p, core, peer).wait_send()
        sib_copy(p, z).wait_send()
        cross_copy(p, core, z).wait_send()
        return 0

    lax.fori_loop(0, PASSES, drain, 0)


def local(
    n_dp, n_camp, row_factors, col_factors, prices, spend_target, step_sizes, eligible, counts
):
    row_blocks, slots = eligible.shape
    col_blocks = prices.shape[0] // BLOCK
    n_z = n_dp // 2
    side = math.isqrt(n_camp)
    chunk = col_blocks // 2 // n_z
    chunks = row_blocks // CHUNK
    wide = 256
    dma = pltpu.SemaphoreType.DMA
    vmem = pltpu.VMEM
    spec = pl.BlockSpec(memory_space=pltpu.VMEM)
    smem = pl.BlockSpec(memory_space=pltpu.SMEM)
    hbm = pl.BlockSpec(memory_space=pltpu.HBM)
    rows_t = row_factors.T
    index, tiles, lead_tiles, lead_rows = pl.pallas_call(
        functools.partial(gather_kernel, col_blocks),
        out_shape=(
            jax.ShapeDtypeStruct((8, wide), jnp.int32),
            jax.ShapeDtypeStruct((row_blocks, RANK, 2 * BLOCK), BF16),
            jax.ShapeDtypeStruct((LEADS, RANK, LEAD_SLOTS * BLOCK), BF16),
            jax.ShapeDtypeStruct((LEADS, RANK, BLOCK), BF16),
        ),
        in_specs=[hbm] * 4,
        out_specs=(spec,) * 4,
        scratch_shapes=[
            vmem((slots, row_blocks), jnp.int32),
            vmem((1, row_blocks), jnp.int32),
            vmem(rows_t.shape, BF16),
            vmem((RANK, col_blocks * BLOCK), BF16),
            pltpu.SMEM((8, wide), jnp.int32),
            dma((5,)),
        ],
        compiler_params=pltpu.CompilerParams(vmem_limit_bytes=60 * 1024 * 1024),
    )(eligible.T, counts.reshape(1, row_blocks), rows_t, col_factors.T)
    per_z = (PASSES, n_z, chunk, BLOCK)
    square = vmem((BLOCK, BLOCK), F32)
    new_prices, norms = pl.pallas_call(
        functools.partial(kernel, n_z, side),
        out_shape=(
            jax.ShapeDtypeStruct((col_blocks, BLOCK), F32),
            jax.ShapeDtypeStruct((row_blocks, BLOCK), F32),
        ),
        in_specs=[hbm] * 6 + [smem, hbm],
        out_specs=(spec, spec),
        scratch_shapes=[
            vmem(rows_t.shape, BF16),
            vmem(tiles.shape, BF16),
            vmem(lead_tiles.shape, BF16),
            vmem(lead_rows.shape, BF16),
            vmem((col_blocks, BLOCK), F32),
            vmem((8, wide), jnp.int32),
            vmem((col_blocks, wide), BF16),
            vmem((wide, col_blocks), BF16),
            vmem((wide, BLOCK), F32),
            vmem((row_blocks, 2 * BLOCK), F32),
            vmem((LEADS, LEAD_SLOTS * BLOCK), F32),
            vmem((row_blocks, BLOCK, 2 * BLOCK), F32),
            vmem((LEADS, BLOCK, LEAD_SLOTS * BLOCK), F32),
            vmem((row_blocks, BLOCK, 2 * BLOCK), F32),
            vmem((LEADS, BLOCK, LEAD_SLOTS * BLOCK), F32),
            vmem((CHUNK, BLOCK, BLOCK), F32),
            vmem((LEADS, BLOCK, BLOCK), F32),
            square,
            square,
            square,
            square,
            square,
            vmem((PASSES, row_blocks, BLOCK), F32),
            vmem((PASSES, n_camp, row_blocks, BLOCK), F32),
            vmem((wide, BLOCK), F32),
            vmem((PASSES, col_blocks, BLOCK), F32),
            vmem(per_z, F32),
            vmem(per_z, F32),
            vmem(per_z, F32),
            vmem((PASSES + 1, col_blocks, BLOCK), F32),
            dma((7,)),
            dma((PASSES, chunks, n_camp)),
            dma((PASSES, chunks, n_camp)),
        ]
        + [dma((PASSES, n_z))] * 8,
        compiler_params=pltpu.CompilerParams(
            collective_id=0, has_side_effects=True, vmem_limit_bytes=56 * 1024 * 1024
        ),
    )(
        rows_t,
        tiles,
        lead_tiles,
        lead_rows,
        prices.reshape(col_blocks, BLOCK),
        spend_target.reshape(col_blocks, BLOCK),
        step_sizes,
        index,
    )
    return new_prices.reshape(-1), norms.reshape(-1)


def solution(mesh):
    placed = (P("dp", None), P("camp", None), P("camp"), P("camp"), P(), P("dp", None), P("dp"))
    return jax.shard_map(
        functools.partial(local, mesh.shape["dp"], mesh.shape["camp"]),
        mesh=mesh,
        in_specs=placed,
        out_specs=(P("camp"), P("dp")),
        check_vma=False,
    )
```

time: 142 us -> 104 us (0.73)
  Pallas kernels: 136 us -> 100 us
  local copies, waits for them, and re-layouts: 5.95 us -> 3.04 us
    pallas_call x1, Pallas kernels: 134 us -> 96.2 us  [local(): pl.pallas_call(functools.partial(kernel, n_z, side), out_shape=(jax.Shape...]
    unnamed x18 -> x2, local copies, waits for them, and re-layouts: 5.95 us -> 3.04 us
    pallas_call x1, Pallas kernels: 1.91 us -> 4.02 us  [local(): pl.pallas_call(functools.partial(gather_kernel, col_blocks), out_shape=(j...]
where the time goes in v2:
time: 104 us
  Pallas kernels  100 us (96%)
  local copies, waits for them, and re-layouts  3.04 us (3%)
    pallas_call x1, Pallas kernels, local(): pl.pallas_call(functools.partial(kernel, n_z, side), out_shape=(jax.Shape...  96.2 us
    pallas_call x1, Pallas kernels, local(): pl.pallas_call(functools.partial(gather_kernel, col_blocks), out_shape=(j...  4.02 us
    unnamed x2, local copies, waits for them, and re-layouts  3.04 us

profile of v2, /device:TPU:1, one launch (start us, length us, event | category | flops | bytes accessed | tf_op | source)
XLA Modules:
  0.0 103.9 jit_solution(14627124918013894603)
XLA Ops:
  0.6 4.0 %shard_map.86 = (s32[8,256]{1,0:T(8,128)}, bf16[64,32,256]{2,1,0:T(8,128)(2,1)}, bf16[8,32,1024]{2,1,0:T(8,128)(2,1)}, bf16[8,32,128]{2,1,0:T(8,128)(2,1)}) custom-call(s32[32,64]{1,0:T(8,128)} %bitcast.15, s32[1,64]{1,0:T(1,128)} %bitcast.16, bf16[32,8192]{1,0:T(8,128)(2,1)} %bitcast.9, bf16[32,65536]{1,0:T(8,128)(2,1)} %bitcast.8), custom_call_target="tpu_custom_call" | custom-call | tf_op jit(solution)/shard_map/pallas_call | solution.py:574
  4.7 96.2 %shard_map.87 = (f32[512,128]{1,0:T(8,128)}, f32[64,128]{1,0:T(8,128)}) custom-call(bf16[32,8192]{1,0:T(8,128)(2,1)} %bitcast.10, bf16[64,32,256]{2,1,0:T(8,128)(2,1)} %get-tuple-element.8.tile_hbm, bf16[8,32,1024]{2,1,0:T(8,128)(2,1)} %get-tuple-element.9.lead_tile_hbm, bf16[8,32,128]{2,1,0:T(8,128)(2,1)} %get-tuple-element.10.lead_row_hbm, ...), custom_call_target="tpu_custom_call" | custom-call | tf_op jit(solution)/shard_map/pallas_call | solution.py:596
  100.9 1.7 %copy.11 = f32[65536]{0:T(1024)} copy(f32[65536]{0:T(1024)} %bitcast.13) | data formatting | bytes 524288
  102.6 1.4 %copy.12 = f32[8192]{0:T(1024)} copy(f32[8192]{0:T(1024)} %bitcast.14) | data formatting | bytes 65536

commit v3 on v2

--- a/solution.py
+++ b/solution.py
@@ -19,7 +19,7 @@
 SCALE = math.log2(math.e) / 0.3
 LN2 = math.log(2.0)
 DEAD = 1e30
-CHUNK = 16
+CHUNK = 32
 
 
 def pieces(x):
@@ -180,22 +180,16 @@
 def kernel(
     n_z,
     side,
-    row_hbm,
-    tile_hbm,
-    lead_tile_hbm,
-    lead_row_hbm,
-    price_hbm,
-    spend_hbm,
-    step_ref,
-    idx_hbm,
-    out_price,
-    out_norm,
     row_ref,
     tile_ref,
     lead_tile_ref,
     lead_row_ref,
+    price_ref,
     spend_ref,
+    step_ref,
     idx_ref,
+    out_price,
+    out_norm,
     sel,
     selt,
     bias,
@@ -220,7 +214,6 @@
     z_out,
     z_in,
     prices,
-    load_sem,
     row_send,
     row_recv,
     sib_send,
@@ -246,23 +239,6 @@
     chunk = half // n_z
     n_camp = side * side
 
-    loads = [
-        pltpu.make_async_copy(src, dst, load_sem.at[i])
-        for i, (src, dst) in enumerate(
-            (
-                (idx_hbm, idx_ref),
-                (price_hbm, prices.at[0]),
-                (row_hbm, row_ref),
-                (tile_hbm, tile_ref),
-                (lead_row_hbm, lead_row_ref),
-                (lead_tile_hbm, lead_tile_ref),
-                (spend_hbm, spend_ref),
-            )
-        )
-    ]
-    for load in loads:
-        load.start()
-
     hops = [min(k, side - k) for k in range(side)]
     camp_peers = [
         lax.rem(x + dx, side) * side + lax.rem(y + dy, side)
@@ -282,7 +258,6 @@
         )
     pl.semaphore_signal(barrier, inc=1, device_id=(sibling, camp), device_id_type=MESH)
 
-    loads[0].wait()
     block_id = idx_ref[0:1, :]
     valid = idx_ref[1:2, :]
     wide = block_id.shape[1]
@@ -302,29 +277,22 @@
             jnp.where(ok > 0.5, 0.0, DEAD), (BLOCK, BLOCK)
         )
 
-    loads[2].wait()
-    loads[3].wait()
-
     def score(b, _):
         at = pl.multiple_of(b * BLOCK, BLOCK)
         s_ref[b] = mm_tn(row_ref[:, pl.ds(at, BLOCK)], tile_ref[b]) * SCALE
         return 0
 
-    lax.fori_loop(0, row_blocks, score, 0, unroll=8)
-    loads[4].wait()
-    loads[5].wait()
+    lax.fori_loop(0, row_blocks, score, 0, unroll=32)
 
     def score_lead(k, _):
         sl_ref[k] = mm_tn(lead_row_ref[k], lead_tile_ref[k]) * SCALE
         return 0
 
-    lax.fori_loop(0, LEADS, score_lead, 0, unroll=2)
+    lax.fori_loop(0, LEADS, score_lead, 0, unroll=8)
 
     parts[...] = jnp.zeros_like(parts)
     turn_ref[...] = jnp.zeros_like(turn_ref)
-    loads[1].wait()
-    loads[6].wait()
-    pl.semaphore_wait(barrier, (n_camp - 1) + (n_z - 1) + 1)
+    prices[0] = price_ref[...]
 
     lane = lax.broadcasted_iota(jnp.int32, (BLOCK, BLOCK), 1)
 
@@ -451,11 +419,16 @@
             lse = l_ref[rows, :]
             lse_ref[p, rows, :] = lse
             row_in[p, camp, rows, :] = lse
+
+            @pl.when((p == 0) & (c == 0))
+            def _():
+                pl.semaphore_wait(barrier, (n_camp - 1) + (n_z - 1) + 1)
+
             for peer in camp_peers:
                 row_copy(p, c, lse_ref, row_in, peer, camp).start()
             return 0
 
-        lax.fori_loop(0, chunks, visit, 0)
+        lax.fori_loop(0, chunks, visit, 0, unroll=True)
 
         @pl.when(p == 0)
         def _():
@@ -478,12 +451,20 @@
             l_ref[...] = weight
             turned = pltpu.roll(weight, lax.rem(BLOCK - c * CHUNK, BLOCK), 1)
             first, second = [], []
-            for u in range(CHUNK):
-                part = jnp.sum(
-                    e_ref[c * CHUNK + u] * turned[:, u : u + 1], axis=0, keepdims=True
-                )
-                first.append(part[:, 0:BLOCK])
-                second.append(part[:, BLOCK:])
+            whi = turned.astype(BF16)
+            wmid = (turned - whi.astype(F32)).astype(BF16)
+            terms = jnp.concatenate([whi, wmid], axis=1)
+            pair = lax.rem(lax.broadcasted_iota(jnp.int32, (BLOCK, 2 * BLOCK), 1), BLOCK) // 2
+            ri = lax.broadcasted_iota(jnp.int32, (2 * BLOCK, 2 * BLOCK), 0)
+            ci = lax.broadcasted_iota(jnp.int32, (2 * BLOCK, 2 * BLOCK), 1)
+            spread = jnp.where(lax.rem(ri, 2) == ci // BLOCK, 1.0, 0.0).astype(BF16)
+            for u in range(0, CHUNK, 2):
+                w2 = mm(jnp.where(pair == u // 2, terms, jnp.zeros_like(terms)), spread)
+                for v in range(2):
+                    w = w2[:, v * BLOCK : (v + 1) * BLOCK]
+                    e = e_ref[c * CHUNK + u + v]
+                    first.append(jnp.sum(e[:, 0:BLOCK] * w, axis=0, keepdims=True))
+                    second.append(jnp.sum(e[:, BLOCK:] * w, axis=0, keepdims=True))
             parts[rows, :] = jnp.concatenate(first, axis=0)
             parts[pl.ds(pl.multiple_of(row_blocks + c * CHUNK, CHUNK), CHUNK), :] = (
                 jnp.concatenate(second, axis=0)
@@ -574,10 +555,10 @@
     index, tiles, lead_tiles, lead_rows = pl.pallas_call(
         functools.partial(gather_kernel, col_blocks),
         out_shape=(
-            jax.ShapeDtypeStruct((8, wide), jnp.int32),
-            jax.ShapeDtypeStruct((row_blocks, RANK, 2 * BLOCK), BF16),
-            jax.ShapeDtypeStruct((LEADS, RANK, LEAD_SLOTS * BLOCK), BF16),
-            jax.ShapeDtypeStruct((LEADS, RANK, BLOCK), BF16),
+            vmem((8, wide), jnp.int32),
+            vmem((row_blocks, RANK, 2 * BLOCK), BF16),
+            vmem((LEADS, RANK, LEAD_SLOTS * BLOCK), BF16),
+            vmem((LEADS, RANK, BLOCK), BF16),
         ),
         in_specs=[hbm] * 4,
         out_specs=(spec,) * 4,
@@ -596,18 +577,12 @@
     new_prices, norms = pl.pallas_call(
         functools.partial(kernel, n_z, side),
         out_shape=(
-            jax.ShapeDtypeStruct((col_blocks, BLOCK), F32),
-            jax.ShapeDtypeStruct((row_blocks, BLOCK), F32),
+            vmem((col_blocks, BLOCK), F32),
+            vmem((row_blocks, BLOCK), F32),
         ),
-        in_specs=[hbm] * 6 + [smem, hbm],
+        in_specs=[spec] * 6 + [smem, spec],
         out_specs=(spec, spec),
         scratch_shapes=[
-            vmem(rows_t.shape, BF16),
-            vmem(tiles.shape, BF16),
-            vmem(lead_tiles.shape, BF16),
-            vmem(lead_rows.shape, BF16),
-            vmem((col_blocks, BLOCK), F32),
-            vmem((8, wide), jnp.int32),
             vmem((col_blocks, wide), BF16),
             vmem((wide, col_blocks), BF16),
             vmem((wide, BLOCK), F32),
@@ -632,13 +607,12 @@
             vmem(per_z, F32),
             vmem(per_z, F32),
             vmem((PASSES + 1, col_blocks, BLOCK), F32),
-            dma((7,)),
             dma((PASSES, chunks, n_camp)),
             dma((PASSES, chunks, n_camp)),
         ]
         + [dma((PASSES, n_z))] * 8,
         compiler_params=pltpu.CompilerParams(
-            collective_id=0, has_side_effects=True, vmem_limit_bytes=56 * 1024 * 1024
+            collective_id=0, has_side_effects=True, vmem_limit_bytes=48 * 1024 * 1024
         ),
     )(
         rows_t,

time: 104 us -> 96.7 us (0.930)
  Pallas kernels: 100 us -> 94.6 us
  local copies, waits for them, and re-layouts: 3.04 us -> 1.35 us
    pallas_call x2, Pallas kernels: 100 us -> 94.6 us  [the longest x1 91.6 us: local(): pl.pallas_call(functools.partial(kernel, n_z, side), out_shape=(vmem((col...]
    unnamed x2 -> x10, local copies, waits for them, and re-layouts: 3.04 us -> 1.35 us
where the time goes in v3:
time: 96.7 us; the launch traced here: 96.6 us
  Pallas kernels  94.6 us (98%)
  local copies, waits for them, and re-layouts  1.35 us (1%)
    pallas_call x1, Pallas kernels, local(): pl.pallas_call(functools.partial(kernel, n_z, side), out_shape=(vmem((col...  91.6 us
    pallas_call x1, Pallas kernels, local(): pl.pallas_call(functools.partial(gather_kernel, col_blocks), out_shape=(v...  2.95 us

profile of v3, /device:TPU:1, one launch (start us, length us, event | category | flops | bytes accessed | tf_op | source)
XLA Modules:
  0.0 96.6 jit_solution(9230795367156381617)
XLA Ops:
  0.6 0.0 copy-start.3
  0.6 0.0 copy-start.2
  0.7 0.0 copy-start.1
  0.7 0.0 copy-start
  0.7 2.9 %shard_map.86 = (s32[8,256]{1,0:T(8,128)S(1)}, bf16[64,32,256]{2,1,0:T(8,128)(2,1)S(1)}, bf16[8,32,1024]{2,1,0:T(8,128)(2,1)S(1)}, bf16[8,32,128]{2,1,0:T(8,128)(2,1)S(1)}) custom-call(s32[32,64]{1,0:T(8,128)} %bitcast.15, s32[1,64]{1,0:T(1,128)} %bitcast.16, bf16[32,8192]{1,0:T(8,128)(2,1)} %bitcast.10, bf16[32,65536]{1,0:T(8,128)(2,1)} %bitcast.14), custom_call_target="tpu_custom_call" | custom-call | tf_op jit(solution)/shard_map/pallas_call | solution.py:555
  3.6 0.0 copy-done.3
  3.6 0.0 copy-done.2
  3.6 0.0 copy-done.1
  3.7 0.0 copy-done
  3.7 91.6 %shard_map.87 = (f32[512,128]{1,0:T(8,128)S(1)}, f32[64,128]{1,0:T(8,128)S(1)}) custom-call(bf16[32,8192]{1,0:T(8,128)(2,1)S(1)} %bitcast.11, bf16[64,32,256]{2,1,0:T(8,128)(2,1)S(1)} %get-tuple-element.8.tile_ref, bf16[8,32,1024]{2,1,0:T(8,128)(2,1)S(1)} %get-tuple-element.9.lead_tile_ref, bf16[8,32,128]{2,1,0:T(8,128)(2,1)S(1)} %get-tuple-element.10.lead_row_ref, ...), custom_call_target="tpu_custom_call" | custom-call | tf_op jit(solution)/shard_map/pallas_call | solution.py:577
  95.3 0.7 copy.11
  96.0 0.6 copy.12
Async XLA Ops:
  0.6 3.0 %copy-start.3 = (f32[3]{0:T(128)S(1)}, f32[3]{0:T(128)}, u32[]{:S(2)}) copy-start(f32[3]{0:T(128)} %step_ref.1) | copy-start | bytes 40
  0.6 3.0 %copy-start.2 = (f32[65536]{0:T(1024)S(1)}, f32[65536]{0:T(1024)}, u32[]{:S(2)}) copy-start(f32[65536]{0:T(1024)} %param.10) | copy-start | bytes 786436
  0.7 3.0 %copy-start.1 = (f32[65536]{0:T(1024)S(1)}, f32[65536]{0:T(1024)}, u32[]{:S(2)}) copy-start(f32[65536]{0:T(1024)} %param.9) | copy-start | bytes 786436
  0.7 3.0 %copy-start = (bf16[8192,32]{0,1:T(8,128)(2,1)S(1)}, bf16[8192,32]{0,1:T(8,128)(2,1)}, u32[]{:S(2)}) copy-start(bf16[8192,32]{0,1:T(8,128)(2,1)} %param.7) | copy-start | bytes 1572868

commit v4 on v3

--- a/solution.py
+++ b/solution.py
@@ -43,8 +43,11 @@
 
 
 def exact_pick(select, x):
-    hi, mid, low = pieces(x)
-    out = mm(select, jnp.concatenate([hi, mid, low], axis=1))
+    return pick_terms(select, jnp.concatenate(pieces(x), axis=1))
+
+
+def pick_terms(select, terms):
+    out = mm(select, terms)
     return out[:, :BLOCK] + out[:, BLOCK : 2 * BLOCK] + out[:, 2 * BLOCK :]
 
 
@@ -357,6 +360,21 @@
             device_id_type=MESH,
         )
 
+    def drain(p):
+        for c in range(chunks):
+            for peer in camp_peers:
+                row_copy(p, c, lse_ref, row_in, peer, camp).wait_send()
+        for peer in z_peers:
+            sib_copy(p, peer).wait_send()
+            z_copy(p, peer, z).wait_send()
+        sib_copy(p, z).wait_send()
+
+    def drain_prices(p):
+        for peer in z_peers:
+            price_copy(p, peer, z).wait_send()
+            cross_copy(p, core, peer).wait_send()
+        cross_copy(p, core, z).wait_send()
+
     def one_pass(p, _):
         picked = exact_pick(selt[...], prices[p] * SCALE) + bias[...]
         pg[:, 0:BLOCK] = picked[0:row_blocks]
@@ -387,7 +405,7 @@
                 )
             return 0
 
-        lax.fori_loop(0, LEADS, visit_lead, 0, unroll=2)
+        lax.fori_loop(0, LEADS, visit_lead, 0, unroll=8)
 
         def add_lead(k, _):
             place = place_of(k)
@@ -400,6 +418,7 @@
 
         def visit(c, _):
             m_all = jnp.zeros((BLOCK, BLOCK), F32)
+            l_all = jnp.zeros((BLOCK, BLOCK), F32)
             for u in range(CHUNK):
                 b = c * CHUNK + u
                 logit = s_ref[b] - pg[pl.ds(b, 1), :]
@@ -409,11 +428,14 @@
                 e_ref[b] = e
                 sum_ref[u] = e[:, 0:BLOCK] + e[:, BLOCK:]
                 m_all = jnp.where(lane == b, m, m_all)
+                if u >= 2:
+                    l = jnp.sum(sum_ref[u - 2], axis=1, keepdims=True)
+                    l_all = jnp.where(lane == b - 2, l, l_all)
+            for u in range(CHUNK - 2, CHUNK):
+                l = jnp.sum(sum_ref[u], axis=1, keepdims=True)
+                l_all = jnp.where(lane == c * CHUNK + u, l, l_all)
             m_ref[...] = m_ref[...] + m_all
-            l_all = ll_ref[...]
-            for u in range(CHUNK):
-                l = jnp.sum(sum_ref[u], axis=1, keepdims=True)
-                l_all = l_all + jnp.where(lane == c * CHUNK + u, l, 0.0)
+            l_all = l_all + ll_ref[...]
             l_ref[...] = (m_ref[...] + jnp.log2(jnp.maximum(l_all, 1e-37))).T
             rows = pl.ds(pl.multiple_of(c * CHUNK, CHUNK), CHUNK)
             lse = l_ref[rows, :]
@@ -429,6 +451,10 @@
             return 0
 
         lax.fori_loop(0, chunks, visit, 0, unroll=True)
+
+        @pl.when(p > 0)
+        def _():
+            drain_prices(p - 1)
 
         @pl.when(p == 0)
         def _():
@@ -471,7 +497,8 @@
             )
             return 0
 
-        lax.fori_loop(0, chunks, weigh, 0)
+        for c in range(chunks):
+            weigh(c, 0)
 
         def weigh_lead(k, _):
             place = place_of(k)
@@ -483,12 +510,17 @@
                 ]
             return 0
 
-        lax.fori_loop(0, LEADS, weigh_lead, 0, unroll=4)
-
-        cols[p] = exact_pick(sel[...], parts[...])
+        for k in range(LEADS):
+            weigh_lead(k, 0)
+
+        terms = jnp.concatenate(pieces(parts[...]), axis=1)
+        away = pl.ds(pl.multiple_of((1 - core) * half, half), half)
+        home = pl.ds(pl.multiple_of(core * half, half), half)
+        cols[p, away, :] = pick_terms(sel[away, :], terms)
         for peer in z_peers:
             sib_copy(p, peer).start()
         sib_copy(p, z).start()
+        cols[p, home, :] = pick_terms(sel[home, :], terms)
         for peer in z_peers:
             sib_copy(p, peer).wait_recv()
             z_out[p, peer] = cols[p, price_rows(core, peer), :] + sib_in[p, peer]
@@ -505,6 +537,7 @@
         for peer in z_peers:
             price_copy(p, peer, z).start()
         cross_copy(p, core, z).start()
+        drain(p)
         for peer in z_peers[::-1]:
             price_copy(p, peer, peer).wait_recv()
             cross_copy(p, core, peer).start()
@@ -517,23 +550,7 @@
     out_price[...] = prices[PASSES]
     out_norm[...] = turn_ref[0:row_blocks, :] * LN2
 
-    def drain(p, _):
-        def drain_rows(c, _):
-            for peer in camp_peers:
-                row_copy(p, c, lse_ref, row_in, peer, camp).wait_send()
-            return 0
-
-        lax.fori_loop(0, chunks, drain_rows, 0)
-        for peer in z_peers:
-            sib_copy(p, peer).wait_send()
-            z_copy(p, peer, z).wait_send()
-            price_copy(p, peer, z).wait_send()
-            cross_copy(p, core, peer).wait_send()
-        sib_copy(p, z).wait_send()
-        cross_copy(p, core, z).wait_send()
-        return 0
-
-    lax.fori_loop(0, PASSES, drain, 0)
+    drain_prices(PASSES - 1)
 
 
 def local(

time: 96.7 us -> 94.3 us (0.975)
  Pallas kernels: 94.6 us -> 92.1 us
    pallas_call x1, Pallas kernels: 91.6 us -> 89.2 us  [local(): pl.pallas_call(functools.partial(kernel, n_z, side), out_shape=(vmem((col...]
where the time goes in v4:
time: 94.3 us; the launch traced here: 94.2 us
  Pallas kernels  92.1 us (98%)
  local copies, waits for them, and re-layouts  1.35 us (1%)
    pallas_call x1, Pallas kernels, local(): pl.pallas_call(functools.partial(kernel, n_z, side), out_shape=(vmem((col...  89.2 us
    pallas_call x1, Pallas kernels, local(): pl.pallas_call(functools.partial(gather_kernel, col_blocks), out_shape=(v...  2.95 us

profile of v4, /device:TPU:1, one launch (start us, length us, event | category | flops | bytes accessed | tf_op | source)
XLA Modules:
  0.0 94.2 jit_solution(3810940807133678849)
XLA Ops:
  0.6 0.0 copy-start.3
  0.6 0.0 copy-start.2
  0.7 0.0 copy-start.1
  0.7 0.0 copy-start
  0.7 2.9 %shard_map.86 = (s32[8,256]{1,0:T(8,128)S(1)}, bf16[64,32,256]{2,1,0:T(8,128)(2,1)S(1)}, bf16[8,32,1024]{2,1,0:T(8,128)(2,1)S(1)}, bf16[8,32,128]{2,1,0:T(8,128)(2,1)S(1)}) custom-call(s32[32,64]{1,0:T(8,128)} %bitcast.15, s32[1,64]{1,0:T(1,128)} %bitcast.16, bf16[32,8192]{1,0:T(8,128)(2,1)} %bitcast.10, bf16[32,65536]{1,0:T(8,128)(2,1)} %bitcast.14), custom_call_target="tpu_custom_call" | custom-call | tf_op jit(solution)/shard_map/pallas_call | solution.py:572
  3.6 0.0 copy-done.3
  3.6 0.0 copy-done.2
  3.6 0.0 copy-done.1
  3.7 0.0 copy-done
  3.7 89.2 %shard_map.87 = (f32[512,128]{1,0:T(8,128)S(1)}, f32[64,128]{1,0:T(8,128)S(1)}) custom-call(bf16[32,8192]{1,0:T(8,128)(2,1)S(1)} %bitcast.11, bf16[64,32,256]{2,1,0:T(8,128)(2,1)S(1)} %get-tuple-element.8.tile_ref, bf16[8,32,1024]{2,1,0:T(8,128)(2,1)S(1)} %get-tuple-element.9.lead_tile_ref, bf16[8,32,128]{2,1,0:T(8,128)(2,1)S(1)} %get-tuple-element.10.lead_row_ref, ...), custom_call_target="tpu_custom_call" | custom-call | tf_op jit(solution)/shard_map/pallas_call | solution.py:594
  92.9 0.7 copy.11
  93.6 0.6 copy.12
Async XLA Ops:
  0.6 3.0 %copy-start.3 = (f32[3]{0:T(128)S(1)}, f32[3]{0:T(128)}, u32[]{:S(2)}) copy-start(f32[3]{0:T(128)} %step_ref.1) | copy-start | bytes 40
  0.6 3.0 %copy-start.2 = (f32[65536]{0:T(1024)S(1)}, f32[65536]{0:T(1024)}, u32[]{:S(2)}) copy-start(f32[65536]{0:T(1024)} %param.10) | copy-start | bytes 786436
  0.7 3.0 %copy-start.1 = (f32[65536]{0:T(1024)S(1)}, f32[65536]{0:T(1024)}, u32[]{:S(2)}) copy-start(f32[65536]{0:T(1024)} %param.9) | copy-start | bytes 786436
  0.7 3.0 %copy-start = (bf16[8192,32]{0,1:T(8,128)(2,1)S(1)}, bf16[8192,32]{0,1:T(8,128)(2,1)}, u32[]{:S(2)}) copy-start(bf16[8192,32]{0,1:T(8,128)(2,1)} %param.7) | copy-start | bytes 1572868

commit v5 on v4

--- a/solution.py
+++ b/solution.py
@@ -19,7 +19,7 @@
 SCALE = math.log2(math.e) / 0.3
 LN2 = math.log(2.0)
 DEAD = 1e30
-CHUNK = 32
+CHUNKS = ((0, 24), (24, 40))
 
 
 def pieces(x):
@@ -236,7 +236,7 @@
     y = lax.rem(camp, side)
     sibling = 2 * z + 1 - core
     row_blocks = s_ref.shape[0]
-    chunks = row_blocks // CHUNK
+    chunks = len(CHUNKS)
     col_blocks = spend_ref.shape[0]
     half = col_blocks // 2
     chunk = half // n_z
@@ -253,9 +253,13 @@
     z_peers = [lax.rem(z + k, n_z) for k in far_first(n_z)]
 
     barrier = pltpu.get_barrier_semaphore()
+    for peer in z_peers[0:1]:
+        pl.semaphore_signal(
+            barrier, inc=1, device_id=(2 * peer + core, camp), device_id_type=MESH
+        )
     for peer in camp_peers:
         pl.semaphore_signal(barrier, inc=1, device_id=(dp, peer), device_id_type=MESH)
-    for peer in z_peers:
+    for peer in z_peers[1:]:
         pl.semaphore_signal(
             barrier, inc=1, device_id=(2 * peer + core, camp), device_id_type=MESH
         )
@@ -308,7 +312,7 @@
         return pl.ds(pl.multiple_of(of_core * half + peer * chunk, chunk), chunk)
 
     def row_copy(p, c, src, dst, peer, slot):
-        rows = pl.ds(pl.multiple_of(c * CHUNK, CHUNK), CHUNK)
+        rows = pl.ds(*CHUNKS[c])
         return pltpu.make_async_remote_copy(
             src_ref=src.at[p, rows],
             dst_ref=dst.at[p, slot, rows],
@@ -416,11 +420,12 @@
         lax.fori_loop(0, LEADS, add_lead, 0, unroll=8)
         m_ref[...] = ml_ref[...]
 
-        def visit(c, _):
+        def visit(c):
+            start, size = CHUNKS[c]
             m_all = jnp.zeros((BLOCK, BLOCK), F32)
             l_all = jnp.zeros((BLOCK, BLOCK), F32)
-            for u in range(CHUNK):
-                b = c * CHUNK + u
+            for u in range(size):
+                b = start + u
                 logit = s_ref[b] - pg[pl.ds(b, 1), :]
                 top = jnp.maximum(logit[:, 0:BLOCK], logit[:, BLOCK:])
                 m = jnp.maximum(jnp.max(top, axis=1, keepdims=True), 0.0)
@@ -431,26 +436,28 @@
                 if u >= 2:
                     l = jnp.sum(sum_ref[u - 2], axis=1, keepdims=True)
                     l_all = jnp.where(lane == b - 2, l, l_all)
-            for u in range(CHUNK - 2, CHUNK):
+            for u in range(size - 2, size):
                 l = jnp.sum(sum_ref[u], axis=1, keepdims=True)
-                l_all = jnp.where(lane == c * CHUNK + u, l, l_all)
+                l_all = jnp.where(lane == start + u, l, l_all)
             m_ref[...] = m_ref[...] + m_all
             l_all = l_all + ll_ref[...]
             l_ref[...] = (m_ref[...] + jnp.log2(jnp.maximum(l_all, 1e-37))).T
-            rows = pl.ds(pl.multiple_of(c * CHUNK, CHUNK), CHUNK)
+            rows = pl.ds(start, size)
             lse = l_ref[rows, :]
             lse_ref[p, rows, :] = lse
             row_in[p, camp, rows, :] = lse
 
-            @pl.when((p == 0) & (c == 0))
-            def _():
-                pl.semaphore_wait(barrier, (n_camp - 1) + (n_z - 1) + 1)
+            if c == 0:
+
+                @pl.when(p == 0)
+                def _():
+                    pl.semaphore_wait(barrier, (n_camp - 1) + (n_z - 1) + 1)
 
             for peer in camp_peers:
                 row_copy(p, c, lse_ref, row_in, peer, camp).start()
-            return 0
-
-        lax.fori_loop(0, chunks, visit, 0, unroll=True)
+
+        for c in range(chunks):
+            visit(c)
 
         @pl.when(p > 0)
         def _():
@@ -465,8 +472,9 @@
                 0.0,
             ).astype(BF16)
 
-        def weigh(c, _):
-            rows = pl.ds(pl.multiple_of(c * CHUNK, CHUNK), CHUNK)
+        def weigh(c):
+            start, size = CHUNKS[c]
+            rows = pl.ds(start, size)
             for peer in camp_peers[::-1]:
                 row_copy(p, c, lse_ref, row_in, peer, peer).wait_recv()
             every = row_in[p, :, rows, :]
@@ -475,7 +483,7 @@
             turn_ref[rows, :] = top + jnp.log2(total)
             weight = jnp.exp2(m_ref[...] - turn_ref[...].T)
             l_ref[...] = weight
-            turned = pltpu.roll(weight, lax.rem(BLOCK - c * CHUNK, BLOCK), 1)
+            turned = pltpu.roll(weight, BLOCK - start, 1) if start else weight
             first, second = [], []
             whi = turned.astype(BF16)
             wmid = (turned - whi.astype(F32)).astype(BF16)
@@ -484,21 +492,20 @@
             ri = lax.broadcasted_iota(jnp.int32, (2 * BLOCK, 2 * BLOCK), 0)
             ci = lax.broadcasted_iota(jnp.int32, (2 * BLOCK, 2 * BLOCK), 1)
             spread = jnp.where(lax.rem(ri, 2) == ci // BLOCK, 1.0, 0.0).astype(BF16)
-            for u in range(0, CHUNK, 2):
+            for u in range(0, size, 2):
                 w2 = mm(jnp.where(pair == u // 2, terms, jnp.zeros_like(terms)), spread)
                 for v in range(2):
                     w = w2[:, v * BLOCK : (v + 1) * BLOCK]
-                    e = e_ref[c * CHUNK + u + v]
+                    e = e_ref[start + u + v]
                     first.append(jnp.sum(e[:, 0:BLOCK] * w, axis=0, keepdims=True))
                     second.append(jnp.sum(e[:, BLOCK:] * w, axis=0, keepdims=True))
             parts[rows, :] = jnp.concatenate(first, axis=0)
-            parts[pl.ds(pl.multiple_of(row_blocks + c * CHUNK, CHUNK), CHUNK), :] = (
+            parts[pl.ds(row_blocks + start, size), :] = (
                 jnp.concatenate(second, axis=0)
             )
-            return 0
 
         for c in range(chunks):
-            weigh(c, 0)
+            weigh(c)
 
         def weigh_lead(k, _):
             place = place_of(k)
@@ -561,7 +568,7 @@
     n_z = n_dp // 2
     side = math.isqrt(n_camp)
     chunk = col_blocks // 2 // n_z
-    chunks = row_blocks // CHUNK
+    chunks = len(CHUNKS)
     wide = 256
     dma = pltpu.SemaphoreType.DMA
     vmem = pltpu.VMEM
@@ -609,7 +616,7 @@
             vmem((LEADS, BLOCK, LEAD_SLOTS * BLOCK), F32),
             vmem((row_blocks, BLOCK, 2 * BLOCK), F32),
             vmem((LEADS, BLOCK, LEAD_SLOTS * BLOCK), F32),
-            vmem((CHUNK, BLOCK, BLOCK), F32),
+            vmem((max(size for _, size in CHUNKS), BLOCK, BLOCK), F32),
             vmem((LEADS, BLOCK, BLOCK), F32),
             square,
             square,

time: 94.3 us -> 93.7 us (level)
  no operation moved by 1% of the time
where the time goes in v5:
time: 93.7 us; the launch traced here: 93.6 us
  Pallas kernels  91.5 us (98%)
  local copies, waits for them, and re-layouts  1.35 us (1%)
    pallas_call x1, Pallas kernels, local(): pl.pallas_call(functools.partial(kernel, n_z, side), out_shape=(vmem((col...  88.6 us
    pallas_call x1, Pallas kernels, local(): pl.pallas_call(functools.partial(gather_kernel, col_blocks), out_shape=(v...  2.95 us

profile of v5, /device:TPU:1, one launch (start us, length us, event | category | flops | bytes accessed | tf_op | source)
XLA Modules:
  0.0 93.6 jit_solution(16183180111695629406)
XLA Ops:
  0.6 0.0 copy-start.3
  0.6 0.0 copy-start.2
  0.7 0.0 copy-start.1
  0.7 0.0 copy-start
  0.7 2.9 %shard_map.86 = (s32[8,256]{1,0:T(8,128)S(1)}, bf16[64,32,256]{2,1,0:T(8,128)(2,1)S(1)}, bf16[8,32,1024]{2,1,0:T(8,128)(2,1)S(1)}, bf16[8,32,128]{2,1,0:T(8,128)(2,1)S(1)}) custom-call(s32[32,64]{1,0:T(8,128)} %bitcast.15, s32[1,64]{1,0:T(1,128)} %bitcast.16, bf16[32,8192]{1,0:T(8,128)(2,1)} %bitcast.10, bf16[32,65536]{1,0:T(8,128)(2,1)} %bitcast.14), custom_call_target="tpu_custom_call" | custom-call | tf_op jit(solution)/shard_map/pallas_call | solution.py:579
  3.6 0.0 copy-done.3
  3.6 0.0 copy-done.2
  3.6 0.0 copy-done.1
  3.7 0.0 copy-done
  3.7 88.6 %shard_map.87 = (f32[512,128]{1,0:T(8,128)S(1)}, f32[64,128]{1,0:T(8,128)S(1)}) custom-call(bf16[32,8192]{1,0:T(8,128)(2,1)S(1)} %bitcast.11, bf16[64,32,256]{2,1,0:T(8,128)(2,1)S(1)} %get-tuple-element.8.tile_ref, bf16[8,32,1024]{2,1,0:T(8,128)(2,1)S(1)} %get-tuple-element.9.lead_tile_ref, bf16[8,32,128]{2,1,0:T(8,128)(2,1)S(1)} %get-tuple-element.10.lead_row_ref, ...), custom_call_target="tpu_custom_call" | custom-call | tf_op jit(solution)/shard_map/pallas_call | solution.py:601
  92.2 0.7 copy.11
  93.0 0.6 copy.12
Async XLA Ops:
  0.6 3.0 %copy-start.3 = (f32[3]{0:T(128)S(1)}, f32[3]{0:T(128)}, u32[]{:S(2)}) copy-start(f32[3]{0:T(128)} %step_ref.1) | copy-start | bytes 40
  0.6 3.0 %copy-start.2 = (f32[65536]{0:T(1024)S(1)}, f32[65536]{0:T(1024)}, u32[]{:S(2)}) copy-start(f32[65536]{0:T(1024)} %param.10) | copy-start | bytes 786436
  0.7 3.0 %copy-start.1 = (f32[65536]{0:T(1024)S(1)}, f32[65536]{0:T(1024)}, u32[]{:S(2)}) copy-start(f32[65536]{0:T(1024)} %param.9) | copy-start | bytes 786436
  0.7 3.0 %copy-start = (bf16[8192,32]{0,1:T(8,128)(2,1)S(1)}, bf16[8192,32]{0,1:T(8,128)(2,1)}, u32[]{:S(2)}) copy-start(bf16[8192,32]{0,1:T(8,128)(2,1)} %param.7) | copy-start | bytes 1572868
